TPU v7x, 256 devices: a whole 4x4x8 slice. The times are simulated.
256 devices in a mesh: dp: 8 (over z), expert: 32 (over y, x, core).
Axes of the slice: x: 4, y: 4, z: 8, core: 2. Of those that a mesh axis runs over, the one named last changes fastest.
Arguments:
- inputs: bfloat16 [32768, 2048], P(('dp', 'expert')), may hold values from -6 to 6
- out_grad: bfloat16 [32768, 2048], P(('dp', 'expert')), may hold values from -6 to 6
- route_weights: bfloat16 [32768, 8], P(('dp', 'expert')), may hold values from 0.019897461 to 0.5
- routes: int32 [32768, 8], P(('dp', 'expert')), may hold values from 0 to 63, all different within a row; in each aligned block of 128 rows (0 to 127, 128 to 255, ...) at most 18 rows name the same one
- response_counts: int32 [256], P(('dp', 'expert')), may hold values from 1 to 128, 16384 in all
- gate_weight: bfloat16 [64, 2048, 384], P('expert'), may hold values from -0.125 to 0.125
- up_weight: bfloat16 [64, 2048, 384], P('expert'), may hold values from -0.125 to 0.125
- down_weight: bfloat16 [64, 384, 2048], P('expert'), may hold values from -0.3125 to 0.3125
Outputs:
- in_grad: bfloat16 [32768, 2048], P(('dp', 'expert'))
- gate_grad: bfloat16 [64, 2048, 384], P('expert', 'dp')
- up_grad: bfloat16 [64, 2048, 384], P('expert', 'dp')
- down_grad: bfloat16 [64, 384, 2048], P('expert', None, 'dp')
- route_weight_grad: bfloat16 [32768, 8], P(('dp', 'expert'))
Inputs may be any that keep to these rules, and one draw needn't show every extreme that they name: `routes`: among the 128 tokens of one device, no expert is named by more than 18 slots, a bound that some block reaches. A token names 8 different experts.
All inputs are finite; a program needn't handle non-finite values. No bound on the sum of `response_counts` on one device may be relied on, other than what follows from the above.
Results may differ from a plain program's by a relative error of at most 0.019.
Values may be sent and summed in bfloat16 or wider, within the bound.
A program may use at most 128 MiB of HBM per device.

v0:
```python
import functools

import jax
import jax.numpy as jnp
from jax import lax
from jax.experimental import pallas as pl
from jax.experimental.pallas import tpu as pltpu
from jax.sharding import PartitionSpec as P

F32 = jnp.float32
BF16 = jnp.bfloat16
I32 = jnp.int32
CELL = 16
EXTRA = 2
SLABS = CELL // EXTRA
VMEM_LIMIT = 56 * 1024 * 1024


def iota(shape, dim):
    return lax.broadcasted_iota(I32, shape, dim)


def mm(a, b, ca=1, cb=0):
    return lax.dot_general(a, b, (((ca,), (cb,)), ((), ())), preferred_element_type=F32)


def cell_tables(routes_t, local, local_count, owners):
    top_k, tokens = routes_t.shape
    wanted = iota((owners, tokens), 0) * local_count + local
    names = jnp.zeros((owners, tokens), F32)
    for k in range(top_k):
        names = names + jnp.where(routes_t[k : k + 1, :] == wanted, 1.0, 0.0)
    before = jnp.where(iota((tokens, tokens), 0) < iota((tokens, tokens), 1), 1.0, 0.0)
    rank = mm(names.astype(BF16), before.astype(BF16))
    rank = jnp.where(names > 0.5, rank, -1.0)
    rows = owners * CELL
    spread = jnp.where(iota((rows, owners), 0) // CELL == iota((rows, owners), 1), 1.0, 0.0)
    spread = spread.astype(BF16)
    rank_rows = mm(spread, rank.astype(BF16)).astype(I32)
    place = iota((rows, tokens), 0) % CELL
    whole = rank_rows == place
    cut = rank_rows == CELL + place % EXTRA
    return wanted, spread, place, whole, cut


def pack_kernel(local, local_count, owners, routes_ref, weights_ref, count_ref, x_ref, dy_ref, out_ref):
    top_k, tokens = routes_ref.shape
    width = x_ref.shape[1]
    slab = width // SLABS
    routes_t = routes_ref[...]
    wanted, spread, place, whole, cut = cell_tables(routes_t, local, local_count, owners)
    combine = jnp.zeros((owners, tokens), F32)
    for k in range(top_k):
        combine = combine + jnp.where(
            routes_t[k : k + 1, :] == wanted, weights_ref[k : k + 1, :].astype(F32), 0.0
        )
    combine_rows = mm(spread, combine.astype(BF16))
    live = iota((1, tokens), 1) >= tokens - count_ref[0]
    pick_x = jnp.where(whole, 1.0, 0.0).astype(BF16)
    pick_dy = jnp.where(whole & live, 1.0, 0.0).astype(BF16)
    out_ref[:, :width] = mm(pick_x, x_ref[...]).astype(BF16)
    out_ref[:, width : 2 * width] = mm(pick_dy, dy_ref[...]).astype(BF16)
    cut_x, cut_dy = 0.0, 0.0
    for j in range(SLABS):
        here = cut & (place // EXTRA == j)
        columns = pl.ds(j * slab, slab)
        cut_x = cut_x + mm(jnp.where(here, 1.0, 0.0).astype(BF16), x_ref[:, columns])
        cut_dy = cut_dy + mm(jnp.where(here & live, 1.0, 0.0).astype(BF16), dy_ref[:, columns])
    out_ref[:, 2 * width : 2 * width + slab] = cut_x.astype(BF16)
    out_ref[:, 2 * width + slab : 2 * width + 2 * slab] = cut_dy.astype(BF16)
    whole_weight = jnp.sum(jnp.where(whole, combine_rows, 0.0), axis=1, keepdims=True)
    cut_weight = jnp.sum(jnp.where(cut, combine_rows, 0.0), axis=1, keepdims=True)
    lane = iota((owners * CELL, 128), 1)
    out_ref[:, 2 * width + 2 * slab :] = jnp.where(lane < 64, whole_weight, cut_weight).astype(BF16)


def expert_kernel(
    groups, grad_scale, recv_ref, wg_ref, wu_ref, wd_ref, grads_ref, back_ref,
    x_all, dy_all, gu_grad, hidden_all,
):
    rows = recv_ref.shape[0]
    width, units = wg_ref.shape
    owners = rows // CELL
    extra = owners * EXTRA
    total = rows + extra
    slab = width // SLABS
    r = iota((extra, rows), 1)
    q = iota((extra, rows), 0)
    x_all[:rows, :] = recv_ref[:, :width]
    dy_all[:rows, :] = recv_ref[:, width : 2 * width]
    cut_x = recv_ref[:, 2 * width : 2 * width + slab]
    cut_dy = recv_ref[:, 2 * width + slab : 2 * width + 2 * slab]
    weight_block = recv_ref[:, 2 * width + 2 * slab :]

    def joiner(j):
        source = q // EXTRA * CELL + j * EXTRA + q % EXTRA
        return jnp.where(r == source, 1.0, 0.0).astype(BF16)

    for j in range(SLABS):
        columns = pl.ds(j * slab, slab)
        x_all[rows:, columns] = mm(joiner(j), cut_x).astype(BF16)
        dy_all[rows:, columns] = mm(joiner(j), cut_dy).astype(BF16)
    weight_whole = weight_block[:, 0:1].astype(F32)
    weight_cut = mm(joiner(0), weight_block)[:, 64:65]
    weight = jnp.concatenate([weight_whole, weight_cut], axis=0)

    step = total // 3
    probs = []
    for i in range(3):
        here = pl.ds(i * step, step)
        x = x_all[here, :]
        dy = dy_all[here, :]
        gate_pre = mm(x, wg_ref[...])
        up_pre = mm(x, wu_ref[...])
        raw = mm(dy, wd_ref[...], 1, 1)
        sig = jax.nn.sigmoid(gate_pre)
        activated = gate_pre * sig
        slope = sig * (1.0 + gate_pre * (1.0 - sig))
        hidden = (activated * up_pre).astype(BF16)
        probs.append(jnp.sum(hidden.astype(F32) * raw, axis=1, keepdims=True))
        w = weight[i * step : (i + 1) * step, :]
        pushed = w * raw
        hidden_all[here, :] = hidden
        gu_grad[here, :units] = (pushed * up_pre * slope).astype(BF16)
        gu_grad[here, units:] = (pushed * activated).astype(BF16)
        dy_all[here, :] = (w * dy.astype(F32)).astype(BF16)

    part = width // groups
    block = grads_ref.shape[0] // groups
    side = grads_ref.shape[1]
    for g in range(groups):
        columns = pl.ds(g * part, part)
        gu = (grad_scale * mm(x_all[:, columns], gu_grad[...], 0, 0)).astype(BF16)
        for s in range(2 * units // side):
            grads_ref[pl.ds(g * block + s * part, part), :] = gu[:, s * side : (s + 1) * side]
        down = grad_scale * mm(hidden_all[...], dy_all[:, columns], 0, 0)
        grads_ref[pl.ds(g * block + 2 * units // side * part, units), :] = down.astype(BF16)

    prob = jnp.concatenate(probs, axis=0)
    cut_back = jnp.zeros((rows, slab), F32)
    r_t = iota((rows, extra), 0)
    q_t = iota((rows, extra), 1)
    half = rows // 2
    for i in range(2):
        here = pl.ds(i * half, half)
        dx = mm(gu_grad[here, :units], wg_ref[...], 1, 1) + mm(gu_grad[here, units:], wu_ref[...], 1, 1)
        back_ref[here, :width] = dx.astype(BF16)
    here = pl.ds(rows, extra)
    dx = mm(gu_grad[here, :units], wg_ref[...], 1, 1) + mm(gu_grad[here, units:], wu_ref[...], 1, 1)
    dx = dx.astype(BF16)
    for j in range(SLABS):
        source = q_t // EXTRA * CELL + j * EXTRA + q_t % EXTRA
        splitter = jnp.where(r_t == source, 1.0, 0.0).astype(BF16)
        cut_back = cut_back + mm(splitter, dx[:, j * slab : (j + 1) * slab])
    back_ref[:, width : width + slab] = cut_back.astype(BF16)
    same = (r_t // CELL == q_t // EXTRA) & (r_t % EXTRA == q_t % EXTRA)
    prob_cut = jnp.broadcast_to(prob[rows:, :], (extra, 128)).astype(BF16)
    prob_cut = mm(jnp.where(same, 1.0, 0.0).astype(BF16), prob_cut)
    lane = iota((rows, 128), 1)
    back_ref[:, width + slab :] = jnp.where(lane < 64, prob[:rows, :], prob_cut).astype(BF16)


def combine_kernel(local_count, owners, routes_ref, *refs):
    back_refs = refs[:local_count]
    dx_ref, prob_ref = refs[local_count:]
    top_k, tokens = routes_ref.shape
    width = dx_ref.shape[1]
    slab = width // SLABS
    routes_t = routes_ref[...]
    dx = 0.0
    cut_dx = [0.0] * SLABS
    probs = [0.0] * top_k
    for local in range(local_count):
        back_ref = back_refs[local]
        wanted, spread, place, whole, cut = cell_tables(routes_t, local, local_count, owners)
        dx = dx + mm(jnp.where(whole, 1.0, 0.0).astype(BF16), back_ref[:, :width], 0, 0)
        for j in range(SLABS):
            here = jnp.where(cut & (place // EXTRA == j), 1.0, 0.0).astype(BF16)
            cut_dx[j] = cut_dx[j] + mm(here, back_ref[:, width : width + slab], 0, 0)
        block = back_ref[:, width + slab :].astype(F32)
        held = jnp.where(whole, block[:, 0:1], 0.0)
        held = held + jnp.where(cut & (place // EXTRA == 0), block[:, 64:65], 0.0)
        by_owner = mm(spread, held.astype(BF16), 0, 0)
        for k in range(top_k):
            mine = jnp.where(routes_t[k : k + 1, :] == wanted, by_owner, 0.0)
            probs[k] = probs[k] + jnp.sum(mine, axis=0, keepdims=True)
    for j in range(SLABS):
        columns = slice(j * slab, (j + 1) * slab)
        dx_ref[:, columns] = (dx[:, columns] + cut_dx[j]).astype(BF16)
    for k in range(top_k):
        prob_ref[k : k + 1, :] = probs[k]


def vmem():
    return pl.BlockSpec(memory_space=pltpu.VMEM)


def shards(
    inputs, out_grad, route_weights, routes, response_counts, gate_weight, up_weight, down_weight
):
    tokens, width = inputs.shape
    top_k = routes.shape[1]
    local_count, _, units = gate_weight.shape
    owners = lax.axis_size("expert")
    groups = lax.axis_size("dp")
    grad_scale = (tokens * top_k * groups / local_count) ** (-0.5)
    rows = owners * CELL
    extra = owners * EXTRA
    slab = width // SLABS
    send_width = 2 * width + 2 * slab + 128
    back_width = width + slab + 128
    part = width // groups
    block = (2 * units * part + units * part) // part
    params = pltpu.CompilerParams(vmem_limit_bytes=VMEM_LIMIT)
    routes_t = routes.T
    weights_t = route_weights.T

    def exchange(array):
        cols = array.shape[1]
        return lax.all_to_all(
            array.reshape(owners, CELL, cols), "expert", split_axis=0, concat_axis=0, tiled=True
        ).reshape(rows, cols)

    received = []
    for local in range(local_count):
        packed = pl.pallas_call(
            functools.partial(pack_kernel, local, local_count, owners),
            out_shape=jax.ShapeDtypeStruct((rows, send_width), BF16),
            in_specs=[vmem(), vmem(), pl.BlockSpec(memory_space=pltpu.SMEM), vmem(), vmem()],
            out_specs=vmem(),
            compiler_params=params,
            cost_estimate=pl.CostEstimate(
                flops=4 * rows * tokens * width, bytes_accessed=2 * rows * send_width, transcendentals=0
            ),
            name="pack",
        )(routes_t, weights_t, response_counts, inputs, out_grad)
        received.append(exchange(packed))

    sums, backs = [], []
    for local in range(local_count):
        grads, back = pl.pallas_call(
            functools.partial(expert_kernel, groups, grad_scale),
            out_shape=(
                jax.ShapeDtypeStruct((groups * 3 * units * part // part, part), BF16),
                jax.ShapeDtypeStruct((rows, back_width), BF16),
            ),
            in_specs=[vmem()] * 4,
            out_specs=(vmem(), vmem()),
            scratch_shapes=[
                pltpu.VMEM((rows + extra, width), BF16),
                pltpu.VMEM((rows + extra, width), BF16),
                pltpu.VMEM((rows + extra, 2 * units), BF16),
                pltpu.VMEM((rows + extra, units), BF16),
            ],
            compiler_params=params,
            cost_estimate=pl.CostEstimate(
                flops=16 * (rows + extra) * width * units,
                bytes_accessed=2 * rows * (send_width + back_width) + 12 * width * units,
                transcendentals=(rows + extra) * units,
            ),
            name="expert",
        )(received[local], gate_weight[local], up_weight[local], down_weight[local])
        backs.append(exchange(back))
        sums.append(lax.psum_scatter(grads, "dp", scatter_dimension=0, tiled=True))

    in_grad, prob_t = pl.pallas_call(
        functools.partial(combine_kernel, local_count, owners),
        out_shape=(
            jax.ShapeDtypeStruct((tokens, width), BF16),
            jax.ShapeDtypeStruct((top_k, tokens), F32),
        ),
        in_specs=[vmem()] * (1 + local_count),
        out_specs=(vmem(), vmem()),
        compiler_params=params,
        cost_estimate=pl.CostEstimate(
            flops=4 * rows * tokens * width, bytes_accessed=4 * rows * back_width, transcendentals=0
        ),
        name="combine",
    )(routes_t, *backs)
    route_weight_grad = prob_t.T.astype(BF16)

    gate_grad, up_grad, down_grad = [], [], []
    for total in sums:
        side = total.shape[1]
        pieces = 2 * units // side
        gu = jnp.concatenate([total[s * part : (s + 1) * part] for s in range(pieces)], axis=1)
        gate_grad.append(gu[:, :units])
        up_grad.append(gu[:, units:])
        down_grad.append(total[pieces * part :])
    return (
        in_grad,
        jnp.stack(gate_grad),
        jnp.stack(up_grad),
        jnp.stack(down_grad),
        route_weight_grad,
    )


def solution(mesh):
    tokens = P(("dp", "expert"), None)
    return jax.shard_map(
        shards,
        mesh=mesh,
        in_specs=(
            tokens, tokens, tokens, tokens,
            P(("dp", "expert")),
            P("expert", None, None), P("expert", None, None), P("expert", None, None),
        ),
        out_specs=(
            tokens, P("expert", "dp", None), P("expert", "dp", None), P("expert", None, "dp"), tokens,
        ),
        check_vma=False,
    )
```

profile of v0, /device:TPU:9, one launch (start us, length us, event | category | flops | bytes accessed | tf_op | source)
XLA Modules:
  0.0 282.3 jit_solution(5458934471357342707)
XLA Ops:
  7.8 6.1 %pack.2 = bf16[512,4736]{1,0:T(8,128)(2,1)} custom-call(s32[8,128]{1,0:T(8,128)} %bitcast.43, bf16[8,128]{1,0:T(8,128)(2,1)} %bitcast.46, s32[1]{0:T(128)S(6)} %copy.13.count_ref, bf16[128,2048]{1,0:T(8,128)(2,1)} %x_ref.3, bf16[128,2048]{1,0:T(8,128)(2,1)} %dy_ref.3), custom_call_target="tpu_custom_call" | custom-call | flops 536870912 | bytes 4849664 | tf_op jit(solution)/shard_map/pack/pallas_call | solution.py:226
  13.9 8.2 %all-to-all-start = ((bf16[32,16,4736]{2,1,0:T(8,128)(2,1)}), bf16[32,16,4736]{2,1,0:T(8,128)(2,1)}, u32[]{:S(2)}, u32[]{:S(2)}) async-start(bf16[32,16,4736]{2,1,0:T(8,128)(2,1)} %bitcast.36), calls=%async_computation | async-start | bytes 9699328 | tf_op jit(solution)/shard_map/all_to_all | solution.py:220
  22.1 0.2 reduce-scatter.3.cloned.1.call-start
  22.3 0.0 copy-done
  22.4 0.0 copy-start.1
  22.4 0.0 copy-start.2
  22.4 1.9 slice_bitcast_fusion
  24.3 1.1 copy-done.1
  25.4 1.0 copy-done.2
  26.3 2.7 slice_bitcast_fusion.1
  29.1 49.2 %all-to-all-done = bf16[32,16,4736]{2,1,0:T(8,128)(2,1)} async-done(((bf16[32,16,4736]{2,1,0:T(8,128)(2,1)}), bf16[32,16,4736]{2,1,0:T(8,128)(2,1)}, u32[]{:S(2)}, u32[]{:S(2)}) %all-to-all-start) | async-done | bytes 4849696 | tf_op jit(solution)/shard_map/all_to_all | solution.py:220
  78.3 17.6 %expert.2 = (bf16[9216,256]{1,0:T(8,128)(2,1)}, bf16[512,2432]{1,0:T(8,128)(2,1)}) custom-call(bf16[512,4736]{1,0:T(8,128)(2,1)} %bitcast.3.recv_ref, bf16[2048,384]{1,0:T(8,128)(2,1)} %get-tuple-element.33.wg_ref, bf16[2048,384]{1,0:T(8,128)(2,1)} %get-tuple-element.20.wu_ref, bf16[384,2048]{1,0:T(8,128)(2,1)} %get-tuple-element.18.wd_ref), custom_call_target="tpu_custom_call" | custom-call | flops 7247757312 | bytes 16777216 | tf_op jit(solution)/shard_map/expert/pallas_call | solution.py:241
  96.0 0.0 reduce-scatter.3.cloned.1.call-update
  96.0 0.3 reduce-scatter.5.cloned.1.call-start
  96.2 6.2 %pack.3 = bf16[512,4736]{1,0:T(8,128)(2,1)} custom-call(s32[8,128]{1,0:T(8,128)} %bitcast.44, bf16[8,128]{1,0:T(8,128)(2,1)} %bitcast.47, s32[1]{0:T(128)S(6)} %copy.13.count_ref, bf16[128,2048]{1,0:T(8,128)(2,1)} %x_ref.3, bf16[128,2048]{1,0:T(8,128)(2,1)} %dy_ref.3), custom_call_target="tpu_custom_call" | custom-call | flops 536870912 | bytes 4849664 | tf_op jit(solution)/shard_map/pack/pallas_call | solution.py:226
  102.4 66.5 %all_to_all.20 = bf16[32,16,4736]{2,1,0:T(8,128)(2,1)} all-to-all(bf16[32,16,4736]{2,1,0:T(8,128)(2,1)} %bitcast.37), channel_id=1, replica_groups=mesh['dp'=8,'expert'=32] {'expert'}, dimensions={0} | all-to-all | bytes 9699328 | tf_op jit(solution)/shard_map/all_to_all | solution.py:220
  168.9 17.6 %expert.3 = (bf16[9216,256]{1,0:T(8,128)(2,1)}, bf16[512,2432]{1,0:T(8,128)(2,1)}) custom-call(bf16[512,4736]{1,0:T(8,128)(2,1)} %bitcast.40, bf16[2048,384]{1,0:T(8,128)(2,1)} %get-tuple-element.34.wg_ref, bf16[2048,384]{1,0:T(8,128)(2,1)} %get-tuple-element.19.wu_ref, bf16[384,2048]{1,0:T(8,128)(2,1)} %get-tuple-element.17.wd_ref), custom_call_target="tpu_custom_call" | custom-call | flops 7247757312 | bytes 16777216 | tf_op jit(solution)/shard_map/expert/pallas_call | solution.py:241
  186.5 0.0 reduce-scatter.5.cloned.1.call-update
  186.6 1.7 copy-done.4
  188.2 37.6 %all_to_all.21 = bf16[32,16,2432]{2,1,0:T(8,128)(2,1)} all-to-all(bf16[32,16,2432]{2,1,0:T(8,128)(2,1)S(1)} %bitcast.42), channel_id=1, replica_groups=mesh['dp'=8,'expert'=32] {'expert'}, dimensions={0} | all-to-all | bytes 4980736 | tf_op jit(solution)/shard_map/all_to_all | solution.py:220
  225.9 0.0 copy-done.3
  225.9 36.5 %all_to_all.22 = bf16[32,16,2432]{2,1,0:T(8,128)(2,1)} all-to-all(bf16[32,16,2432]{2,1,0:T(8,128)(2,1)S(1)} %bitcast.41), channel_id=1, replica_groups=mesh['dp'=8,'expert'=32] {'expert'}, dimensions={0} | all-to-all | bytes 4980736 | tf_op jit(solution)/shard_map/all_to_all | solution.py:220
  262.4 5.3 %combine.1 = (bf16[128,2048]{1,0:T(8,128)(2,1)}, f32[8,128]{1,0:T(8,128)}) custom-call(s32[8,128]{1,0:T(8,128)} %bitcast.45, bf16[512,2432]{1,0:T(8,128)(2,1)} %bitcast.39, bf16[512,2432]{1,0:T(8,128)(2,1)} %bitcast.38), custom_call_target="tpu_custom_call" | custom-call | flops 536870912 | bytes 4980736 | tf_op jit(solution)/shard_map/combine/pallas_call | solution.py:266
  267.6 1.3 convert_bitcast_fusion
  268.9 1.1 fusion.4
  270.0 0.0 reduce-scatter.5.cloned.1.call-done
  270.1 1.1 fusion.5
  271.2 0.8 pad_maximum_fusion.1
  272.0 0.8 pad_maximum_fusion
  272.8 0.9 slice_bitcast_fusion.6
  273.7 0.9 slice_bitcast_fusion.7
  274.6 0.8 pad_maximum_fusion.2
  (6 shorter events, 0.1 us)
Async XLA Ops:
  13.9 8.4 %copy-start = (bf16[2,384,2048]{2,1,0:T(8,128)(2,1)S(1)}, bf16[2,384,2048]{2,1,0:T(8,128)(2,1)}, u32[]{:S(2)}) copy-start(bf16[2,384,2048]{2,1,0:T(8,128)(2,1)} %param.15) | copy-start | bytes 9437188
  13.9 64.4 %all-to-all-start = ((bf16[32,16,4736]{2,1,0:T(8,128)(2,1)}), bf16[32,16,4736]{2,1,0:T(8,128)(2,1)}, u32[]{:S(2)}, u32[]{:S(2)}) async-start(bf16[32,16,4736]{2,1,0:T(8,128)(2,1)} %bitcast.36), calls=%async_computation | async-start | bytes 9699328 | tf_op jit(solution)/shard_map/all_to_all | solution.py:220
  22.1 246.8 %reduce-scatter.3.cloned.1.call-start = ((), (), s32[]{:S(2)}) async-start(), calls=%async_computation.6 | async-start | bytes 5308416 | tf_op jit(solution)/shard_map/reduce_scatter | solution.py:264
  22.4 3.0 %copy-start.1 = (bf16[2,2048,384]{2,1,0:T(8,128)(2,1)S(1)}, bf16[2,2048,384]{2,1,0:T(8,128)(2,1)}, u32[]{:S(2)}) copy-start(bf16[2,2048,384]{2,1,0:T(8,128)(2,1)} %param.14) | copy-start | bytes 9437188
  22.4 4.0 %copy-start.2 = (bf16[2,2048,384]{2,1,0:T(8,128)(2,1)S(1)}, bf16[2,2048,384]{2,1,0:T(8,128)(2,1)}, u32[]{:S(2)}) copy-start(bf16[2,2048,384]{2,1,0:T(8,128)(2,1)} %param.13) | copy-start | bytes 9437188
  96.0 174.1 %reduce-scatter.5.cloned.1.call-start = ((), (), s32[]{:S(2)}) async-start(), calls=%async_computation.7 | async-start | bytes 5308416 | tf_op jit(solution)/shard_map/reduce_scatter | solution.py:264
  186.5 1.7 copy-start.4
  188.2 37.6 %copy-start.3 = (bf16[512,2432]{1,0:T(8,128)(2,1)S(1)}, bf16[512,2432]{1,0:T(8,128)(2,1)}, u32[]{:S(2)}) copy-start(bf16[512,2432]{1,0:T(8,128)(2,1)} %get-tuple-element.11) | copy-start | bytes 7471108
Sparse Core Ops, SparseCore 0:
  96.1 62.9 reduce-scatter.2
  186.7 61.3 reduce-scatter.4
where the time goes:
time: 285 us; the launch traced here: 282 us
  blocking collectives  141 us (49%)
  Pallas kernels  52.8 us (19%)
  waiting for transfers between devices  49.3 us (17%)
  between operations  14.8 us (5%)
  local copies, waits for them, and re-layouts  12.4 us (4%)
  starting transfers between devices  8.65 us (3%)
  other arithmetic  3.73 us (1%)
    all_to_all x3, blocking collectives, exchange(): lax.all_to_all(array.reshape(owners, CELL, cols), 'expert', split_axis=0,...  141 us
    all_to_all x1, waiting for transfers between devices, exchange(): lax.all_to_all(array.reshape(owners, CELL, cols), 'expert', split_axis=0,...  49.2 us
    pallas_call x2, Pallas kernels, shards(): pl.pallas_call(functools.partial(expert_kernel, groups, grad_scale), out_...  35.2 us
    pallas_call x2, Pallas kernels, shards(): pl.pallas_call(functools.partial(pack_kernel, local, local_count, owners)...  12.3 us
    all_to_all x1, starting transfers between devices, exchange(): lax.all_to_all(array.reshape(owners, CELL, cols), 'expert', split_axis=0,...  8.17 us
  transfers between devices with their start and end apart: 3, of which 1 were waited for; matrix products, arithmetic and copies ran while one was open for 2% of the time, Pallas kernels for 10%

commit v1 on v0

v1 whole, which is shorter than its diff:
```python
import functools

import jax
import jax.numpy as jnp
from jax import lax
from jax.experimental import pallas as pl
from jax.experimental.pallas import tpu as pltpu
from jax.sharding import PartitionSpec as P

F32 = jnp.float32
BF16 = jnp.bfloat16
I32 = jnp.int32
CELL = 16
EXTRA = 2
SLABS = CELL // EXTRA
VMEM_LIMIT = 60 * 1024 * 1024
MESH = pl.DeviceIdType.MESH


def iota(shape, dim):
    return lax.broadcasted_iota(I32, shape, dim)


def mm(a, b, ca=1, cb=0):
    return lax.dot_general(a, b, (((ca,), (cb,)), ((), ())), preferred_element_type=F32)


def cell_tables(routes_t, local, local_count, owners):
    top_k, tokens = routes_t.shape
    wanted = iota((owners, tokens), 0) * local_count + local
    names = jnp.zeros((owners, tokens), F32)
    for k in range(top_k):
        names = names + jnp.where(routes_t[k : k + 1, :] == wanted, 1.0, 0.0)
    before = jnp.where(iota((tokens, tokens), 0) < iota((tokens, tokens), 1), 1.0, 0.0)
    rank = mm(names.astype(BF16), before.astype(BF16))
    rank = jnp.where(names > 0.5, rank, -1.0)
    rows = owners * CELL
    spread = jnp.where(iota((rows, owners), 0) // CELL == iota((rows, owners), 1), 1.0, 0.0)
    spread = spread.astype(BF16)
    rank_rows = mm(spread, rank.astype(BF16)).astype(I32)
    place = iota((rows, tokens), 0) % CELL
    whole = rank_rows == place
    cut = rank_rows == CELL + place % EXTRA
    return wanted, spread, place, whole, cut


def pack(local, local_count, owners, routes_ref, weights_ref, count_ref, x_ref, dy_ref, out_ref):
    top_k, tokens = routes_ref.shape
    width = x_ref.shape[1]
    slab = width // SLABS
    routes_t = routes_ref[...]
    wanted, spread, place, whole, cut = cell_tables(routes_t, local, local_count, owners)
    combine = jnp.zeros((owners, tokens), F32)
    for k in range(top_k):
        combine = combine + jnp.where(
            routes_t[k : k + 1, :] == wanted, weights_ref[k : k + 1, :].astype(F32), 0.0
        )
    combine_rows = mm(spread, combine.astype(BF16))
    live = iota((1, tokens), 1) >= tokens - count_ref[0]
    pick_x = jnp.where(whole, 1.0, 0.0).astype(BF16)
    pick_dy = jnp.where(whole & live, 1.0, 0.0).astype(BF16)
    out_ref[:, :width] = mm(pick_x, x_ref[...]).astype(BF16)
    out_ref[:, width : 2 * width] = mm(pick_dy, dy_ref[...]).astype(BF16)
    cut_x, cut_dy = 0.0, 0.0
    for j in range(SLABS):
        here = cut & (place // EXTRA == j)
        columns = pl.ds(j * slab, slab)
        cut_x = cut_x + mm(jnp.where(here, 1.0, 0.0).astype(BF16), x_ref[:, columns])
        cut_dy = cut_dy + mm(jnp.where(here & live, 1.0, 0.0).astype(BF16), dy_ref[:, columns])
    out_ref[:, 2 * width : 2 * width + slab] = cut_x.astype(BF16)
    out_ref[:, 2 * width + slab : 2 * width + 2 * slab] = cut_dy.astype(BF16)
    whole_weight = jnp.sum(jnp.where(whole, combine_rows, 0.0), axis=1, keepdims=True)
    cut_weight = jnp.sum(jnp.where(cut, combine_rows, 0.0), axis=1, keepdims=True)
    lane = iota((owners * CELL, 128), 1)
    out_ref[:, 2 * width + 2 * slab :] = jnp.where(lane < 64, whole_weight, cut_weight).astype(BF16)


def whole_kernel(
    grad_scale,
    routes_ref, weights_ref, count_ref, x_ref, dy_ref, wg_ref, wu_ref, wd_ref,
    dx_ref, prob_ref, sums_ref, recv_ref,
    send, x_all, dy_all, side, gu_grad, hidden_all, w_gu, w_down, grads, flow_r, flow_l,
    back_send, back_recv,
    load_sem, own_sem, send_sem, recv_sem, back_own_sem, back_send_sem, back_recv_sem,
    weight_sem, flow_send_sem, flow_recv_sem,
):
    owners, groups = lax.axis_size("expert"), lax.axis_size("dp")
    me, z = lax.axis_index("expert"), lax.axis_index("dp")
    local_count, width, units = wg_ref.shape
    top_k, tokens = routes_ref.shape
    rows = owners * CELL
    extra = owners * EXTRA
    total = rows + extra
    slab = width // SLABS
    half = groups // 2
    block = grads.shape[2]
    top = block // 2
    ring_right = (lax.rem(z + 1, groups), me)
    ring_left = (lax.rem(z + groups - 1, groups), me)
    beside = (z, lax.rem(me + 1, owners))

    def load_weights(local, start):
        copies = [
            pltpu.make_async_copy(wg_ref.at[local], w_gu.at[:, pl.ds(0, units)], weight_sem.at[0]),
            pltpu.make_async_copy(wu_ref.at[local], w_gu.at[:, pl.ds(units, units)], weight_sem.at[1]),
            pltpu.make_async_copy(wd_ref.at[local], w_down, weight_sem.at[2]),
        ]
        for copy in copies:
            if start:
                copy.start()
            else:
                copy.wait()

    def spread_out(source, target, own, sends, recvs, local):
        pltpu.make_async_copy(
            source.at[local, pl.ds(me * CELL, CELL)], target.at[local, pl.ds(me * CELL, CELL)],
            own.at[local],
        ).start()

        def one(i, carry):
            to = lax.rem(me + i, owners)
            pltpu.make_async_remote_copy(
                src_ref=source.at[local, pl.ds(to * CELL, CELL)],
                dst_ref=target.at[local, pl.ds(me * CELL, CELL)],
                send_sem=sends.at[local],
                recv_sem=recvs.at[local],
                device_id=(z, to),
                device_id_type=MESH,
            ).start()
            return carry

        lax.fori_loop(1, owners, one, 0)

    def all_of(source, target, sends, recvs, local):
        most = pl.ds(0, rows - CELL)
        return pltpu.make_async_remote_copy(
            src_ref=source.at[local, most], dst_ref=target.at[local, most],
            send_sem=sends.at[local], recv_sem=recvs.at[local],
            device_id=beside, device_id_type=MESH,
        )

    def wait_own(source, target, own, local):
        pltpu.make_async_copy(
            source.at[local, pl.ds(me * CELL, CELL)], target.at[local, pl.ds(me * CELL, CELL)],
            own.at[local],
        ).wait()

    def hop(local, step, right):
        flow = flow_r if right else flow_l
        way = 0 if right else 1
        if step == 0:
            target = lax.rem(z + (half if right else groups - half), groups)
            part = pl.ds(0 if right else top, top)
            source, landing = grads.at[local, target, part], flow.at[local, 0, part]
        else:
            source, landing = flow.at[local, step - 1], flow.at[local, step]
        return pltpu.make_async_remote_copy(
            src_ref=source, dst_ref=landing,
            send_sem=flow_send_sem.at[local, way, step], recv_sem=flow_recv_sem.at[local, way, step],
            device_id=ring_right if right else ring_left, device_id_type=MESH,
        )

    def add_rows(out, terms):
        count = terms[0].shape[0]
        piece = count // 4

        def one(i, carry):
            here = pl.ds(pl.multiple_of(i * piece, piece), piece)
            value = terms[0][here, :].astype(F32)
            for term in terms[1:]:
                value = value + term[here, :].astype(F32)
            out[here, :] = value.astype(BF16)
            return carry

        lax.fori_loop(0, 4, one, 0)

    def ring_step(local, step):
        for right in (True, False):
            flow = flow_r if right else flow_l
            if step > 0:
                hop(local, step - 1, right).wait_recv()
                away = half - step
                target = lax.rem(z + (away if right else groups - away), groups)
                if step == 1:
                    fresh, rest = (0, top) if right else (top, 0)
                    here, there = pl.ds(fresh, top), pl.ds(rest, top)
                    held = flow.at[local, 0, here]
                    add_rows(held, [held, grads.at[local, target, here]])
                    flow[local, 0, there] = grads[local, target, there]
                else:
                    held = flow.at[local, step - 1]
                    add_rows(held, [held, grads.at[local, target]])
            hop(local, step, right).start()

    def ring_end(local):
        hop(local, half - 1, True).wait_recv()
        hop(local, half - 1, False).wait_recv()
        if half == 1:
            a, b = pl.ds(0, top), pl.ds(top, top)
            add_rows(sums_ref.at[local, a], [grads.at[local, z, a], flow_r.at[local, 0, a]])
            add_rows(sums_ref.at[local, b], [grads.at[local, z, b], flow_l.at[local, 0, b]])
        else:
            last = half - 1
            add_rows(
                sums_ref.at[local],
                [grads.at[local, z], flow_r.at[local, last], flow_l.at[local, last]],
            )

    r = iota((extra, rows), 1)
    q = iota((extra, rows), 0)
    r_t = iota((rows, extra), 0)
    q_t = iota((rows, extra), 1)

    def load_rows(local):
        all_of(send, recv_ref, send_sem, recv_sem, local).wait_recv()
        wait_own(send, recv_ref, own_sem, local)
        copies = [
            pltpu.make_async_copy(
                recv_ref.at[local, :, pl.ds(0, width)], x_all.at[pl.ds(0, rows)], load_sem.at[0]),
            pltpu.make_async_copy(
                recv_ref.at[local, :, pl.ds(width, width)], dy_all.at[pl.ds(0, rows)], load_sem.at[1]),
            pltpu.make_async_copy(
                recv_ref.at[local, :, pl.ds(2 * width, 2 * slab + 128)], side, load_sem.at[2]),
        ]
        for copy in copies:
            copy.start()
        for copy in copies:
            copy.wait()

    def forward(local):
        cut_x, cut_dy, weight_block = side[:, :slab], side[:, slab : 2 * slab], side[:, 2 * slab :]

        def joiner(j):
            source = q // EXTRA * CELL + j * EXTRA + q % EXTRA
            return jnp.where(r == source, 1.0, 0.0).astype(BF16)

        for j in range(SLABS):
            columns = pl.ds(j * slab, slab)
            x_all[rows:, columns] = mm(joiner(j), cut_x).astype(BF16)
            dy_all[rows:, columns] = mm(joiner(j), cut_dy).astype(BF16)
        weight_whole = weight_block[:, 0:1].astype(F32)
        weight_cut = mm(joiner(0), weight_block)[:, 64:65]
        weight = jnp.concatenate([weight_whole, weight_cut], axis=0)
        step = total // 3
        probs = []
        for i in range(3):
            here = pl.ds(i * step, step)
            dy = dy_all[here, :]
            pre = mm(x_all[here, :], w_gu[...])
            gate_pre, up_pre = pre[:, :units], pre[:, units:]
            raw = mm(dy, w_down[...], 1, 1)
            sig = jax.nn.sigmoid(gate_pre)
            activated = gate_pre * sig
            slope = sig * (1.0 + gate_pre * (1.0 - sig))
            hidden = (activated * up_pre).astype(BF16)
            probs.append(jnp.sum(hidden.astype(F32) * raw, axis=1, keepdims=True))
            w = weight[i * step : (i + 1) * step, :]
            pushed = w * raw
            hidden_all[here, :] = hidden
            gu_grad[here, :units] = (pushed * up_pre * slope).astype(BF16)
            gu_grad[here, units:] = (pushed * activated).astype(BF16)
            dy_all[here, :] = (w * dy.astype(F32)).astype(BF16)
        prob = jnp.concatenate(probs, axis=0)
        same = (r_t // CELL == q_t // EXTRA) & (r_t % EXTRA == q_t % EXTRA)
        prob_cut = jnp.broadcast_to(prob[rows:, :], (extra, 128)).astype(BF16)
        prob_cut = mm(jnp.where(same, 1.0, 0.0).astype(BF16), prob_cut)
        lane = iota((rows, 128), 1)
        back_send[local, :, width + slab :] = jnp.where(lane < 64, prob[:rows, :], prob_cut).astype(BF16)

    def weight_grads(local):
        part = width // groups
        pieces = 2 * units // part

        def one(g, carry):
            columns = pl.ds(pl.multiple_of(g * part, part), part)
            gu = (grad_scale * mm(x_all[:, columns], gu_grad[...], 0, 0)).astype(BF16)
            for s in range(pieces):
                grads[local, g, s * part : (s + 1) * part, :] = gu[:, s * part : (s + 1) * part]
            down = grad_scale * mm(hidden_all[...], dy_all[:, columns], 0, 0)
            grads[local, g, pieces * part :, :] = down.astype(BF16)
            return carry

        lax.fori_loop(0, groups, one, 0)

    def input_grads(local):
        piece = rows // 2
        for i in range(2):
            here = pl.ds(i * piece, piece)
            back_send[local, here, :width] = mm(gu_grad[here, :], w_gu[...], 1, 1).astype(BF16)
        dx = mm(gu_grad[rows:, :], w_gu[...], 1, 1).astype(BF16)
        cut_back = 0.0
        for j in range(SLABS):
            source = q_t // EXTRA * CELL + j * EXTRA + q_t % EXTRA
            splitter = jnp.where(r_t == source, 1.0, 0.0).astype(BF16)
            cut_back = cut_back + mm(splitter, dx[:, j * slab : (j + 1) * slab])
        back_send[local, :, width : width + slab] = cut_back.astype(BF16)

    load_weights(0, True)
    barrier = pltpu.get_barrier_semaphore()

    def greet(i, carry):
        pl.semaphore_signal(barrier, inc=1, device_id=(z, lax.rem(me + i, owners)), device_id_type=MESH)
        return carry

    lax.fori_loop(1, owners, greet, 0)
    pl.semaphore_signal(barrier, inc=1, device_id=ring_right, device_id_type=MESH)
    pl.semaphore_signal(barrier, inc=1, device_id=ring_left, device_id_type=MESH)
    pack(0, local_count, owners, routes_ref, weights_ref, count_ref, x_ref, dy_ref, send.at[0])
    pl.semaphore_wait(barrier, owners + 1)
    spread_out(send, recv_ref, own_sem, send_sem, recv_sem, 0)
    pack(1, local_count, owners, routes_ref, weights_ref, count_ref, x_ref, dy_ref, send.at[1])
    all_of(send, recv_ref, send_sem, recv_sem, 0).wait_send()
    spread_out(send, recv_ref, own_sem, send_sem, recv_sem, 1)

    load_weights(0, False)
    load_rows(0)
    forward(0)
    weight_grads(0)
    ring_step(0, 0)
    input_grads(0)
    spread_out(back_send, back_recv, back_own_sem, back_send_sem, back_recv_sem, 0)
    load_weights(1, True)
    for step in range(1, half):
        ring_step(0, step)

    load_weights(1, False)
    load_rows(1)
    forward(1)
    weight_grads(1)
    ring_step(1, 0)
    input_grads(1)
    spread_out(back_send, back_recv, back_own_sem, back_send_sem, back_recv_sem, 1)
    ring_end(0)
    for step in range(1, half):
        ring_step(1, step)
    for local in range(local_count):
        all_of(back_send, back_recv, back_send_sem, back_recv_sem, local).wait_recv()
        wait_own(back_send, back_recv, back_own_sem, local)
    combine(local_count, owners, routes_ref, [back_recv.at[i] for i in range(local_count)], dx_ref, prob_ref)
    ring_end(1)
    all_of(send, recv_ref, send_sem, recv_sem, 1).wait_send()
    for local in range(local_count):
        all_of(back_send, back_recv, back_send_sem, back_recv_sem, local).wait_send()
        for step in range(half):
            hop(local, step, True).wait_send()
            hop(local, step, False).wait_send()


def combine(local_count, owners, routes_ref, back_refs, dx_ref, prob_ref):
    top_k, tokens = routes_ref.shape
    width = dx_ref.shape[1]
    slab = width // SLABS
    routes_t = routes_ref[...]
    dx = 0.0
    cut_dx = [0.0] * SLABS
    probs = [0.0] * top_k
    for local in range(local_count):
        back_ref = back_refs[local]
        wanted, spread, place, whole, cut = cell_tables(routes_t, local, local_count, owners)
        dx = dx + mm(jnp.where(whole, 1.0, 0.0).astype(BF16), back_ref[:, :width], 0, 0)
        for j in range(SLABS):
            here = jnp.where(cut & (place // EXTRA == j), 1.0, 0.0).astype(BF16)
            cut_dx[j] = cut_dx[j] + mm(here, back_ref[:, width : width + slab], 0, 0)
        block = back_ref[:, width + slab :].astype(F32)
        held = jnp.where(whole, block[:, 0:1], 0.0)
        held = held + jnp.where(cut & (place // EXTRA == 0), block[:, 64:65], 0.0)
        by_owner = mm(spread, held.astype(BF16), 0, 0)
        for k in range(top_k):
            mine = jnp.where(routes_t[k : k + 1, :] == wanted, by_owner, 0.0)
            probs[k] = probs[k] + jnp.sum(mine, axis=0, keepdims=True)
    for j in range(SLABS):
        columns = slice(j * slab, (j + 1) * slab)
        dx_ref[:, columns] = (dx[:, columns] + cut_dx[j]).astype(BF16)
    for k in range(top_k):
        prob_ref[k : k + 1, :] = probs[k]


def vmem():
    return pl.BlockSpec(memory_space=pltpu.VMEM)


def shards(
    inputs, out_grad, route_weights, routes, response_counts, gate_weight, up_weight, down_weight
):
    tokens, width = inputs.shape
    top_k = routes.shape[1]
    local_count, _, units = gate_weight.shape
    owners = lax.axis_size("expert")
    groups = lax.axis_size("dp")
    grad_scale = (tokens * top_k * groups / local_count) ** (-0.5)
    rows = owners * CELL
    extra = owners * EXTRA
    slab = width // SLABS
    half = groups // 2
    send_width = 2 * width + 2 * slab + 128
    back_width = width + slab + 128
    part = width // groups
    block = 3 * units
    dma = pltpu.SemaphoreType.DMA
    in_grad, prob_t, sums, _ = pl.pallas_call(
        functools.partial(whole_kernel, grad_scale),
        out_shape=(
            jax.ShapeDtypeStruct((tokens, width), BF16),
            jax.ShapeDtypeStruct((top_k, tokens), F32),
            jax.ShapeDtypeStruct((local_count, block, part), BF16),
            jax.ShapeDtypeStruct((local_count, rows, send_width), BF16),
        ),
        in_specs=[vmem(), vmem(), pl.BlockSpec(memory_space=pltpu.SMEM), vmem(), vmem()]
        + [pl.BlockSpec(memory_space=pl.ANY)] * 3,
        out_specs=(vmem(), vmem(), vmem(), pl.BlockSpec(memory_space=pl.ANY)),
        scratch_shapes=[
            pltpu.VMEM((local_count, rows, send_width), BF16),
            pltpu.VMEM((rows + extra, width), BF16),
            pltpu.VMEM((rows + extra, width), BF16),
            pltpu.VMEM((rows, 2 * slab + 128), BF16),
            pltpu.VMEM((rows + extra, 2 * units), BF16),
            pltpu.VMEM((rows + extra, units), BF16),
            pltpu.VMEM((width, 2 * units), BF16),
            pltpu.VMEM((units, width), BF16),
            pltpu.VMEM((local_count, groups, block, part), BF16),
            pltpu.VMEM((local_count, half, block, part), BF16),
            pltpu.VMEM((local_count, half, block, part), BF16),
            pltpu.VMEM((local_count, rows, back_width), BF16),
            pltpu.VMEM((local_count, rows, back_width), BF16),
            dma((3,)), dma((2,)), dma((2,)), dma((2,)), dma((2,)), dma((2,)), dma((2,)),
            dma((3,)), dma((2, 2, half)), dma((2, 2, half)),
        ],
        compiler_params=pltpu.CompilerParams(
            vmem_limit_bytes=VMEM_LIMIT, collective_id=0, has_side_effects=True
        ),
        name="whole",
    )(routes.T, route_weights.T, response_counts, inputs, out_grad, gate_weight, up_weight, down_weight)
    route_weight_grad = prob_t.T.astype(BF16)

    gate_grad, up_grad, down_grad = [], [], []
    for local in range(local_count):
        total = sums[local]
        side = total.shape[1]
        pieces = 2 * units // side
        gu = jnp.concatenate([total[s * part : (s + 1) * part] for s in range(pieces)], axis=1)
        gate_grad.append(gu[:, :units])
        up_grad.append(gu[:, units:])
        down_grad.append(total[pieces * part :])
    return (
        in_grad,
        jnp.stack(gate_grad),
        jnp.stack(up_grad),
        jnp.stack(down_grad),
        route_weight_grad,
    )


def solution(mesh):
    tokens = P(("dp", "expert"), None)
    return jax.shard_map(
        shards,
        mesh=mesh,
        in_specs=(
            tokens, tokens, tokens, tokens,
            P(("dp", "expert")),
            P("expert", None, None), P("expert", None, None), P("expert", None, None),
        ),
        out_specs=(
            tokens, P("expert", "dp", None), P("expert", "dp", None), P("expert", None, "dp"), tokens,
        ),
        check_vma=False,
    )
```

time: 285 us -> 247 us (0.87)
  Pallas kernels: 52.8 us -> 239 us
  blocking collectives: 141 us -> 0 us
  waiting for transfers between devices: 49.3 us -> 0 us
  between operations: 14.8 us -> 1.31 us
  starting transfers between devices: 8.65 us -> 0 us
  local copies, waits for them, and re-layouts: 12.4 us -> 3.82 us
    pallas_call x5 -> x1, Pallas kernels: 52.8 us -> 239 us  [shards(): pl.pallas_call(functools.partial(whole_kernel, grad_scale), out_shape=(ja...]
    all_to_all x3 -> x0, blocking collectives: 141 us -> none  [exchange(): lax.all_to_all(array.reshape(owners, CELL, cols), 'expert', split_axis=0,...]
    all_to_all x1 -> x0, waiting for transfers between devices: 49.2 us -> none  [exchange(): lax.all_to_all(array.reshape(owners, CELL, cols), 'expert', split_axis=0,...]
    all_to_all x1 -> x0, starting transfers between devices: 8.17 us -> none  [exchange(): lax.all_to_all(array.reshape(owners, CELL, cols), 'expert', split_axis=0,...]
    squeeze x2 -> x0, local copies, waits for them, and re-layouts: 4.65 us -> none  [the longest x1 2.74 us: shards(): up_weight[local]]
    unnamed x10 -> x3, local copies, waits for them, and re-layouts: 3.75 us -> 0.8 us
  transfers between devices with their start and end apart: 3 -> 0, of which waited for: 1 -> 0; matrix products, arithmetic and copies ran while one was open for 2% -> 0% of each run, Pallas kernels for 10% -> 0%
where the time goes in v1:
time: 247 us
  Pallas kernels  239 us (97%)
  local copies, waits for them, and re-layouts  3.82 us (2%)
  other arithmetic  2.99 us (1%)
    pallas_call x1, Pallas kernels, shards(): pl.pallas_call(functools.partial(whole_kernel, grad_scale), out_shape=(ja...  239 us

profile of v1, /device:TPU:9, one launch (start us, length us, event | category | flops | bytes accessed | tf_op | source)
XLA Modules:
  0.0 246.7 jit_solution(1728718969660613523)
XLA Ops:
  1.3 238.6 %whole.1 = (bf16[128,2048]{1,0:T(8,128)(2,1)}, f32[8,128]{1,0:T(8,128)}, bf16[2,1152,256]{2,1,0:T(8,128)(2,1)}, bf16[2,512,4736]{2,1,0:T(8,128)(2,1)}) custom-call(s32[8,128]{1,0:T(8,128)} %bitcast.24, bf16[8,128]{1,0:T(8,128)(2,1)} %bitcast.25, s32[1]{0:T(128)S(6)} %copy.14.count_ref, bf16[128,2048]{1,0:T(8,128)(2,1)} %x_ref.1, bf16[128,2048]{1,0:T(8,128)(2,1)} %dy_ref.1, ...), custom_call_target="tpu_custom_call" | custom-call | tf_op jit(solution)/shard_map/whole/pallas_call | solution.py:400
  239.9 0.0 copy-start
  239.9 1.3 convert_bitcast_fusion
  241.2 1.8 stack.29
  243.0 1.3 slice_bitcast_fusion.1
  244.2 0.1 fusion
  244.3 0.8 pad_maximum_fusion.1
  245.1 0.8 pad_maximum_fusion
  245.9 0.0 copy-done
  245.9 0.8 copy.15
Async XLA Ops:
  239.9 6.0 %copy-start = (bf16[128,2048]{1,0:T(8,128)(2,1)S(1)}, bf16[128,2048]{1,0:T(8,128)(2,1)}, u32[]{:S(2)}) copy-start(bf16[128,2048]{1,0:T(8,128)(2,1)} %get-tuple-element.28) | copy-start | bytes 1572868

commit v2 on v1

--- a/solution.py
+++ b/solution.py
@@ -78,7 +78,7 @@
 def whole_kernel(
     grad_scale,
     routes_ref, weights_ref, count_ref, x_ref, dy_ref, wg_ref, wu_ref, wd_ref,
-    dx_ref, prob_ref, sums_ref, recv_ref,
+    dx_ref, prob_ref, gate_ref, up_ref, down_ref, recv_ref,
     send, x_all, dy_all, side, gu_grad, hidden_all, w_gu, w_down, grads, flow_r, flow_l,
     back_send, back_recv,
     load_sem, own_sem, send_sem, recv_sem, back_own_sem, back_send_sem, back_recv_sem,
@@ -117,19 +117,24 @@
             own.at[local],
         ).start()
 
-        def one(i, carry):
-            to = lax.rem(me + i, owners)
-            pltpu.make_async_remote_copy(
-                src_ref=source.at[local, pl.ds(to * CELL, CELL)],
-                dst_ref=target.at[local, pl.ds(me * CELL, CELL)],
-                send_sem=sends.at[local],
-                recv_sem=recvs.at[local],
-                device_id=(z, to),
-                device_id_type=MESH,
-            ).start()
-            return carry
-
-        lax.fori_loop(1, owners, one, 0)
+        tiles = source.shape[2] // 128
+        pieces = max(1, tiles // 4)
+        for c in range(pieces):
+            low, high = tiles * c // pieces * 128, tiles * (c + 1) // pieces * 128
+
+            def one(i, carry, columns=pl.ds(low, high - low)):
+                to = lax.rem(me + i, owners)
+                pltpu.make_async_remote_copy(
+                    src_ref=source.at[local, pl.ds(to * CELL, CELL), columns],
+                    dst_ref=target.at[local, pl.ds(me * CELL, CELL), columns],
+                    send_sem=sends.at[local],
+                    recv_sem=recvs.at[local],
+                    device_id=(z, to),
+                    device_id_type=MESH,
+                ).start()
+                return carry
+
+            lax.fori_loop(1, owners, one, 0)
 
     def all_of(source, target, sends, recvs, local):
         most = pl.ds(0, rows - CELL)
@@ -193,18 +198,32 @@
             hop(local, step, right).start()
 
     def ring_end(local):
-        hop(local, half - 1, True).wait_recv()
-        hop(local, half - 1, False).wait_recv()
-        if half == 1:
-            a, b = pl.ds(0, top), pl.ds(top, top)
-            add_rows(sums_ref.at[local, a], [grads.at[local, z, a], flow_r.at[local, 0, a]])
-            add_rows(sums_ref.at[local, b], [grads.at[local, z, b], flow_l.at[local, 0, b]])
-        else:
-            last = half - 1
-            add_rows(
-                sums_ref.at[local],
-                [grads.at[local, z], flow_r.at[local, last], flow_l.at[local, last]],
-            )
+        last = half - 1
+        hop(local, last, True).wait_recv()
+        hop(local, last, False).wait_recv()
+        part = width // groups
+        pieces = 2 * units // part
+
+        def summed(low, count):
+            here = pl.ds(low, count)
+            value = grads[local, z, here, :].astype(F32)
+            if half > 1 or low < top:
+                value = value + flow_r[local, last, here, :].astype(F32)
+            if half > 1 or low >= top:
+                value = value + flow_l[local, last, here, :].astype(F32)
+            return value.astype(BF16)
+
+        step = part // 2
+        for i in range(2 * pieces):
+            value = summed(i * step, step)
+            at, here = i // 2 * part, slice(i % 2 * step, (i % 2 + 1) * step)
+            in_gate = max(0, min(part, units - at))
+            if in_gate > 0:
+                gate_ref[local, here, at : at + in_gate] = value[:, :in_gate]
+            if in_gate < part:
+                up_ref[local, here, at + in_gate - units : at + part - units] = value[:, in_gate:]
+        for i in range(units // step):
+            down_ref[local, i * step : (i + 1) * step, :] = summed(pieces * part + i * step, step)
 
     r = iota((extra, rows), 1)
     q = iota((extra, rows), 0)
@@ -271,7 +290,8 @@
         part = width // groups
         pieces = 2 * units // part
 
-        def one(g, carry):
+        def one(k, carry):
+            g = lax.rem(z + half + k, groups)
             columns = pl.ds(pl.multiple_of(g * part, part), part)
             gu = (grad_scale * mm(x_all[:, columns], gu_grad[...], 0, 0)).astype(BF16)
             for s in range(pieces):
@@ -280,7 +300,9 @@
             grads[local, g, pieces * part :, :] = down.astype(BF16)
             return carry
 
-        lax.fori_loop(0, groups, one, 0)
+        one(0, 0)
+        ring_step(local, 0)
+        lax.fori_loop(1, groups, one, 0)
 
     def input_grads(local):
         piece = rows // 2
@@ -316,7 +338,6 @@
     load_rows(0)
     forward(0)
     weight_grads(0)
-    ring_step(0, 0)
     input_grads(0)
     spread_out(back_send, back_recv, back_own_sem, back_send_sem, back_recv_sem, 0)
     load_weights(1, True)
@@ -327,7 +348,6 @@
     load_rows(1)
     forward(1)
     weight_grads(1)
-    ring_step(1, 0)
     input_grads(1)
     spread_out(back_send, back_recv, back_own_sem, back_send_sem, back_recv_sem, 1)
     ring_end(0)
@@ -397,17 +417,19 @@
     part = width // groups
     block = 3 * units
     dma = pltpu.SemaphoreType.DMA
-    in_grad, prob_t, sums, _ = pl.pallas_call(
+    in_grad, prob_t, gate_grad, up_grad, down_grad, _ = pl.pallas_call(
         functools.partial(whole_kernel, grad_scale),
         out_shape=(
             jax.ShapeDtypeStruct((tokens, width), BF16),
             jax.ShapeDtypeStruct((top_k, tokens), F32),
-            jax.ShapeDtypeStruct((local_count, block, part), BF16),
+            jax.ShapeDtypeStruct((local_count, part, units), BF16),
+            jax.ShapeDtypeStruct((local_count, part, units), BF16),
+            jax.ShapeDtypeStruct((local_count, units, part), BF16),
             jax.ShapeDtypeStruct((local_count, rows, send_width), BF16),
         ),
         in_specs=[vmem(), vmem(), pl.BlockSpec(memory_space=pltpu.SMEM), vmem(), vmem()]
         + [pl.BlockSpec(memory_space=pl.ANY)] * 3,
-        out_specs=(vmem(), vmem(), vmem(), pl.BlockSpec(memory_space=pl.ANY)),
+        out_specs=(vmem(), vmem(), vmem(), vmem(), vmem(), pl.BlockSpec(memory_space=pl.ANY)),
         scratch_shapes=[
             pltpu.VMEM((local_count, rows, send_width), BF16),
             pltpu.VMEM((rows + extra, width), BF16),
@@ -431,23 +453,7 @@
         name="whole",
     )(routes.T, route_weights.T, response_counts, inputs, out_grad, gate_weight, up_weight, down_weight)
     route_weight_grad = prob_t.T.astype(BF16)
-
-    gate_grad, up_grad, down_grad = [], [], []
-    for local in range(local_count):
-        total = sums[local]
-        side = total.shape[1]
-        pieces = 2 * units // side
-        gu = jnp.concatenate([total[s * part : (s + 1) * part] for s in range(pieces)], axis=1)
-        gate_grad.append(gu[:, :units])
-        up_grad.append(gu[:, units:])
-        down_grad.append(total[pieces * part :])
-    return (
-        in_grad,
-        jnp.stack(gate_grad),
-        jnp.stack(up_grad),
-        jnp.stack(down_grad),
-        route_weight_grad,
-    )
+    return in_grad, gate_grad, up_grad, down_grad, route_weight_grad
 
 
 def solution(mesh):

time: 247 us -> 196 us (0.79)
  Pallas kernels: 239 us -> 184 us
  local copies, waits for them, and re-layouts: 3.82 us -> 7.21 us
    pallas_call x1, Pallas kernels: 239 us -> 184 us  [shards(): pl.pallas_call(functools.partial(whole_kernel, grad_scale), out_shape=(ja...]
    unnamed x3 -> x4, local copies, waits for them, and re-layouts: 0.8 us -> 7.21 us
where the time goes in v2:
time: 196 us; the launch traced here: 194 us
  Pallas kernels  184 us (94%)
  local copies, waits for them, and re-layouts  7.21 us (4%)
    pallas_call x1, Pallas kernels, shards(): pl.pallas_call(functools.partial(whole_kernel, grad_scale), out_shape=(ja...  184 us
    unnamed x4, local copies, waits for them, and re-layouts  7.21 us

profile of v2, /device:TPU:9, one launch (start us, length us, event | category | flops | bytes accessed | tf_op | source)
XLA Modules:
  0.0 194.1 jit_solution(1614425999886575434)
XLA Ops:
  1.3 184.4 %whole.1 = (bf16[128,2048]{1,0:T(8,128)(2,1)}, f32[8,128]{1,0:T(8,128)}, bf16[2,256,384]{2,1,0:T(8,128)(2,1)}, bf16[2,256,384]{2,1,0:T(8,128)(2,1)}, bf16[2,384,...) custom-call(s32[8,128]{1,0:T(8,128)} %bitcast.4, bf16[8,128]{1,0:T(8,128)(2,1)} %bitcast.5, s32[1]{0:T(128)S(6)} %copy.17.count_ref, ...), custom_call_target="tpu_custom_call" | custom-call | tf_op jit(solution)/shard_map/whole/pallas_call | solution.py:420
  185.7 1.3 convert_bitcast_fusion
  186.9 1.9 copy.18
  188.8 1.8 copy.19
  190.6 1.8 copy.20
  192.3 1.8 copy.21

commit v3 on v2

--- a/solution.py
+++ b/solution.py
@@ -13,7 +13,7 @@
 CELL = 16
 EXTRA = 2
 SLABS = CELL // EXTRA
-VMEM_LIMIT = 60 * 1024 * 1024
+VMEM_LIMIT = 61 * 1024 * 1024
 MESH = pl.DeviceIdType.MESH
 
 
@@ -25,9 +25,9 @@
     return lax.dot_general(a, b, (((ca,), (cb,)), ((), ())), preferred_element_type=F32)
 
 
-def cell_tables(routes_t, local, local_count, owners):
+def cell_tables(routes_t, wanted):
     top_k, tokens = routes_t.shape
-    wanted = iota((owners, tokens), 0) * local_count + local
+    owners = wanted.shape[0]
     names = jnp.zeros((owners, tokens), F32)
     for k in range(top_k):
         names = names + jnp.where(routes_t[k : k + 1, :] == wanted, 1.0, 0.0)
@@ -41,51 +41,52 @@
     place = iota((rows, tokens), 0) % CELL
     whole = rank_rows == place
     cut = rank_rows == CELL + place % EXTRA
-    return wanted, spread, place, whole, cut
-
-
-def pack(local, local_count, owners, routes_ref, weights_ref, count_ref, x_ref, dy_ref, out_ref):
-    top_k, tokens = routes_ref.shape
-    width = x_ref.shape[1]
-    slab = width // SLABS
-    routes_t = routes_ref[...]
-    wanted, spread, place, whole, cut = cell_tables(routes_t, local, local_count, owners)
-    combine = jnp.zeros((owners, tokens), F32)
-    for k in range(top_k):
-        combine = combine + jnp.where(
-            routes_t[k : k + 1, :] == wanted, weights_ref[k : k + 1, :].astype(F32), 0.0
+    return spread, place, whole, cut
+
+
+def pack(wanted, meta, rows_in, out_ref, top):
+    tokens = meta.shape[1]
+    width = rows_in.shape[1]
+    slab = width // 2 // SLABS
+    routes_t = meta[:top, :].astype(F32).astype(I32)
+    weights_t = meta[top:, :].astype(F32)
+    spread, place, whole, cut = cell_tables(routes_t, wanted)
+    combine_weights = jnp.zeros(wanted.shape, F32)
+    for k in range(top):
+        combine_weights = combine_weights + jnp.where(
+            routes_t[k : k + 1, :] == wanted, weights_t[k : k + 1, :], 0.0
         )
-    combine_rows = mm(spread, combine.astype(BF16))
-    live = iota((1, tokens), 1) >= tokens - count_ref[0]
-    pick_x = jnp.where(whole, 1.0, 0.0).astype(BF16)
-    pick_dy = jnp.where(whole & live, 1.0, 0.0).astype(BF16)
-    out_ref[:, :width] = mm(pick_x, x_ref[...]).astype(BF16)
-    out_ref[:, width : 2 * width] = mm(pick_dy, dy_ref[...]).astype(BF16)
-    cut_x, cut_dy = 0.0, 0.0
-    for j in range(SLABS):
-        here = cut & (place // EXTRA == j)
-        columns = pl.ds(j * slab, slab)
-        cut_x = cut_x + mm(jnp.where(here, 1.0, 0.0).astype(BF16), x_ref[:, columns])
-        cut_dy = cut_dy + mm(jnp.where(here & live, 1.0, 0.0).astype(BF16), dy_ref[:, columns])
-    out_ref[:, 2 * width : 2 * width + slab] = cut_x.astype(BF16)
-    out_ref[:, 2 * width + slab : 2 * width + 2 * slab] = cut_dy.astype(BF16)
-    whole_weight = jnp.sum(jnp.where(whole, combine_rows, 0.0), axis=1, keepdims=True)
-    cut_weight = jnp.sum(jnp.where(cut, combine_rows, 0.0), axis=1, keepdims=True)
-    lane = iota((owners * CELL, 128), 1)
-    out_ref[:, 2 * width + 2 * slab :] = jnp.where(lane < 64, whole_weight, cut_weight).astype(BF16)
+    weight_rows = mm(spread, combine_weights.astype(BF16))
+    out_ref[:, :width] = mm(jnp.where(whole, 1.0, 0.0).astype(BF16), rows_in).astype(BF16)
+    picks = [jnp.where(cut & (place // EXTRA == j), 1.0, 0.0).astype(BF16) for j in range(SLABS)]
+    slabs = [
+        jnp.concatenate(
+            [rows_in[:, h * (width // 2) + j * slab : h * (width // 2) + (j + 1) * slab] for h in range(2)],
+            axis=1,
+        )
+        for j in range(SLABS)
+    ]
+    parts = mm(jnp.concatenate(picks, axis=1), jnp.concatenate(slabs, axis=0))
+    out_ref[:, width : width + 2 * slab] = parts.astype(BF16)
+    whole_weight = jnp.sum(jnp.where(whole, weight_rows, 0.0), axis=1, keepdims=True)
+    cut_weight = jnp.sum(jnp.where(cut, weight_rows, 0.0), axis=1, keepdims=True)
+    lane = iota((out_ref.shape[0], 128), 1)
+    out_ref[:, width + 2 * slab :] = jnp.where(lane < 64, whole_weight, cut_weight).astype(BF16)
 
 
 def whole_kernel(
-    grad_scale,
-    routes_ref, weights_ref, count_ref, x_ref, dy_ref, wg_ref, wu_ref, wd_ref,
+    grad_scale, across,
+    routes_ref, meta_ref, count_ref, x_ref, dy_ref, wg_ref, wu_ref, wd_ref,
     dx_ref, prob_ref, gate_ref, up_ref, down_ref, recv_ref,
-    send, x_all, dy_all, side, gu_grad, hidden_all, w_gu, w_down, grads, flow_r, flow_l,
-    back_send, back_recv,
+    stage, meta, send, x_all, dy_all, side, gu_grad, hidden_all, w_gu, w_down, grads, flow_r, flow_l,
+    back_recv,
+    stage_send_sem, stage_recv_sem, meta_send_sem, meta_recv_sem,
     load_sem, own_sem, send_sem, recv_sem, back_own_sem, back_send_sem, back_recv_sem,
     weight_sem, flow_send_sem, flow_recv_sem,
 ):
     owners, groups = lax.axis_size("expert"), lax.axis_size("dp")
     me, z = lax.axis_index("expert"), lax.axis_index("dp")
+    back_send = send.at[0]
     local_count, width, units = wg_ref.shape
     top_k, tokens = routes_ref.shape
     rows = owners * CELL
@@ -98,6 +99,151 @@
     ring_right = (lax.rem(z + 1, groups), me)
     ring_left = (lax.rem(z + groups - 1, groups), me)
     beside = (z, lax.rem(me + 1, owners))
+    half_width = width // 2
+    half_slab = slab // 2
+    up_down = owners // 2 // across
+    y, x, core = me // (2 * across), (me // 2) % across, me % 2
+    sources = (across, up_down)
+    mine = (x, y)
+    targets = (2 * up_down, 2 * across)
+    my_target = (2 * y + core, 2 * x + core)
+    sent_width = (2 * half_width + 2 * half_slab + 128, 2 * half_width + 2 * half_slab)
+    offset = (0, sent_width[0])
+
+    def source_index(way, s):
+        return (y * across + s) * 2 + core if way == 0 else (s * across + x) * 2 + core
+
+    def target_index(way, d):
+        return ((d // 2) * across + x) * 2 + d % 2 if way == 0 else (y * across + d // 2) * 2 + d % 2
+
+    def fill_stage():
+        live = iota((tokens, 1), 0) >= tokens - count_ref[0]
+        for way in range(2):
+            columns = pl.ds(way * half_width, half_width)
+            stage[way, mine[way], :, :half_width] = x_ref[:, columns]
+            dy = jnp.where(live, dy_ref[:, columns].astype(F32), 0.0).astype(BF16)
+            stage[way, mine[way], :, half_width:] = dy
+            meta[way, mine[way]] = meta_ref[...]
+
+    def first_hop():
+        for way in range(2):
+
+            def tell(i, carry, way=way):
+                s = lax.rem(mine[way] + i, sources[way])
+                pltpu.make_async_remote_copy(
+                    src_ref=meta.at[way, mine[way]], dst_ref=meta.at[way, mine[way]],
+                    send_sem=meta_send_sem.at[way], recv_sem=meta_recv_sem.at[way],
+                    device_id=(z, source_index(way, s)), device_id_type=MESH,
+                ).start()
+                return carry
+
+            lax.fori_loop(1, sources[way], tell, 0)
+        pieces = 8
+        size = 2 * half_width // pieces
+        for c in range(pieces):
+            for way in range(2):
+
+                def one(i, carry, way=way, columns=pl.ds(c * size, size)):
+                    s = lax.rem(mine[way] + i, sources[way])
+                    pltpu.make_async_remote_copy(
+                        src_ref=stage.at[way, mine[way], :, columns],
+                        dst_ref=stage.at[way, mine[way], :, columns],
+                        send_sem=stage_send_sem.at[way], recv_sem=stage_recv_sem.at[way],
+                        device_id=(z, source_index(way, s)), device_id_type=MESH,
+                    ).start()
+                    return carry
+
+                lax.fori_loop(1, sources[way], one, 0)
+
+    def first_hop_copies(way):
+        others = pl.ds(0, sources[way] - 1)
+        return [
+            pltpu.make_async_remote_copy(
+                src_ref=array.at[way, others], dst_ref=array.at[way, others],
+                send_sem=sends.at[way], recv_sem=recvs.at[way],
+                device_id=beside, device_id_type=MESH,
+            )
+            for array, sends, recvs in (
+                (meta, meta_send_sem, meta_recv_sem), (stage, stage_send_sem, stage_recv_sem),
+            )
+            if sources[way] > 1
+        ]
+
+    def pack_way(local, way):
+        count = targets[way]
+        wanted = target_index(way, iota((count, tokens), 0)) * local_count + local
+
+        def one(s, carry):
+            here = pl.ds(pl.multiple_of(s * count * CELL, CELL), count * CELL)
+            pack(wanted, meta[way, s], stage[way, s], send.at[local, way, here], meta.shape[2] // 2)
+            return carry
+
+        lax.fori_loop(0, sources[way], one, 0)
+
+    def cell_copy(local, way, s, d, columns):
+        return (
+            send.at[local, way, pl.ds((s * targets[way] + d) * CELL, CELL), columns],
+            recv_ref.at[
+                local, pl.ds(source_index(way, s) * CELL, CELL),
+                pl.ds(offset[way] + columns.start, columns.size),
+            ],
+        )
+
+    def second_hop(local):
+        for way in range(2):
+
+            def keep(s, carry, way=way):
+                a, b = cell_copy(local, way, s, my_target[way], pl.ds(0, sent_width[way]))
+                pltpu.make_async_copy(a, b, own_sem.at[local, way]).start()
+                return carry
+
+            lax.fori_loop(0, sources[way], keep, 0)
+        pieces = 4
+        for c in range(pieces):
+
+            def one(k, carry, ways=(0, 1), c=c):
+                for way in ways:
+                    tiles = sent_width[way] // 128
+                    low, high = tiles * c // pieces * 128, tiles * (c + 1) // pieces * 128
+                    others = targets[way] - 1
+                    d = lax.rem(my_target[way] + 1 + lax.rem(k, others), targets[way])
+                    a, b = cell_copy(local, way, k // others, d, pl.ds(low, high - low))
+                    pltpu.make_async_remote_copy(
+                        src_ref=a, dst_ref=b,
+                        send_sem=send_sem.at[local, way], recv_sem=recv_sem.at[local, way],
+                        device_id=(z, target_index(way, d)), device_id_type=MESH,
+                    ).start()
+                return carry
+
+            counts = [sources[way] * (targets[way] - 1) for way in range(2)]
+            if counts[0] == counts[1]:
+                lax.fori_loop(0, counts[0], one, 0)
+            else:
+                for way in range(2):
+                    lax.fori_loop(0, counts[way], functools.partial(one, ways=(way,)), 0)
+
+    def second_hop_copy(local, way):
+        most = pl.ds(0, sources[way] * (targets[way] - 1) * CELL)
+        return pltpu.make_async_remote_copy(
+            src_ref=send.at[local, way, most, pl.ds(0, sent_width[way])],
+            dst_ref=recv_ref.at[local, most, pl.ds(offset[way], sent_width[way])],
+            send_sem=send_sem.at[local, way], recv_sem=recv_sem.at[local, way],
+            device_id=beside, device_id_type=MESH,
+        )
+
+    def second_hop_sent(local):
+        for way in range(2):
+            second_hop_copy(local, way).wait_send()
+
+    def second_hop_arrived(local):
+        for way in range(2):
+            second_hop_copy(local, way).wait_recv()
+            most = pl.ds(0, sources[way] * CELL)
+            pltpu.make_async_copy(
+                send.at[local, way, most, pl.ds(0, sent_width[way])],
+                recv_ref.at[local, most, pl.ds(offset[way], sent_width[way])],
+                own_sem.at[local, way],
+            ).wait()
 
     def load_weights(local, start):
         copies = [
@@ -150,18 +296,27 @@
             own.at[local],
         ).wait()
 
-    def hop(local, step, right):
+    def hops_of(right, part):
+        return half if right == (part == 0) else half - 1
+
+    chains = [c for c in ((True, 0), (False, 1), (True, 1), (False, 0)) if hops_of(*c) > 0]
+
+    def chain_target(right, part, step):
+        away = hops_of(right, part) - step
+        return lax.rem(z + (away if right else groups - away), groups)
+
+    def hop(local, right, part, step):
         flow = flow_r if right else flow_l
+        here = pl.ds(part * top, top)
+        if step == 0:
+            source = grads.at[local, chain_target(right, part, 0), here]
+        else:
+            source = flow.at[local, step - 1, here]
         way = 0 if right else 1
-        if step == 0:
-            target = lax.rem(z + (half if right else groups - half), groups)
-            part = pl.ds(0 if right else top, top)
-            source, landing = grads.at[local, target, part], flow.at[local, 0, part]
-        else:
-            source, landing = flow.at[local, step - 1], flow.at[local, step]
         return pltpu.make_async_remote_copy(
-            src_ref=source, dst_ref=landing,
-            send_sem=flow_send_sem.at[local, way, step], recv_sem=flow_recv_sem.at[local, way, step],
+            src_ref=source, dst_ref=flow.at[local, step, here],
+            send_sem=flow_send_sem.at[local, way, part, step],
+            recv_sem=flow_recv_sem.at[local, way, part, step],
             device_id=ring_right if right else ring_left, device_id_type=MESH,
         )
 
@@ -180,43 +335,33 @@
         lax.fori_loop(0, 4, one, 0)
 
     def ring_step(local, step):
-        for right in (True, False):
-            flow = flow_r if right else flow_l
-            if step > 0:
-                hop(local, step - 1, right).wait_recv()
-                away = half - step
-                target = lax.rem(z + (away if right else groups - away), groups)
-                if step == 1:
-                    fresh, rest = (0, top) if right else (top, 0)
-                    here, there = pl.ds(fresh, top), pl.ds(rest, top)
-                    held = flow.at[local, 0, here]
-                    add_rows(held, [held, grads.at[local, target, here]])
-                    flow[local, 0, there] = grads[local, target, there]
-                else:
-                    held = flow.at[local, step - 1]
-                    add_rows(held, [held, grads.at[local, target]])
-            hop(local, step, right).start()
+        for right, part in chains:
+            if step < hops_of(right, part):
+                hop(local, right, part, step - 1).wait_recv()
+                held = (flow_r if right else flow_l).at[local, step - 1, pl.ds(part * top, top)]
+                own = grads.at[local, chain_target(right, part, step), pl.ds(part * top, top)]
+                add_rows(held, [held, own])
+                hop(local, right, part, step).start()
 
     def ring_end(local):
-        last = half - 1
-        hop(local, last, True).wait_recv()
-        hop(local, last, False).wait_recv()
+        for right, half_at in chains:
+            hop(local, right, half_at, hops_of(right, half_at) - 1).wait_recv()
         part = width // groups
         pieces = 2 * units // part
 
         def summed(low, count):
             here = pl.ds(low, count)
             value = grads[local, z, here, :].astype(F32)
-            if half > 1 or low < top:
-                value = value + flow_r[local, last, here, :].astype(F32)
-            if half > 1 or low >= top:
-                value = value + flow_l[local, last, here, :].astype(F32)
+            for right, half_at in chains:
+                if half_at == low // top:
+                    flow = flow_r if right else flow_l
+                    value = value + flow[local, hops_of(right, half_at) - 1, here, :].astype(F32)
             return value.astype(BF16)
 
-        step = part // 2
-        for i in range(2 * pieces):
+        step = part // 4
+        for i in range(4 * pieces):
             value = summed(i * step, step)
-            at, here = i // 2 * part, slice(i % 2 * step, (i % 2 + 1) * step)
+            at, here = i // 4 * part, slice(i % 4 * step, (i % 4 + 1) * step)
             in_gate = max(0, min(part, units - at))
             if in_gate > 0:
                 gate_ref[local, here, at : at + in_gate] = value[:, :in_gate]
@@ -225,40 +370,47 @@
         for i in range(units // step):
             down_ref[local, i * step : (i + 1) * step, :] = summed(pieces * part + i * step, step)
 
+    side_width = 2 * half_slab + 128
     r = iota((extra, rows), 1)
     q = iota((extra, rows), 0)
     r_t = iota((rows, extra), 0)
     q_t = iota((rows, extra), 1)
 
     def load_rows(local):
-        all_of(send, recv_ref, send_sem, recv_sem, local).wait_recv()
-        wait_own(send, recv_ref, own_sem, local)
-        copies = [
-            pltpu.make_async_copy(
-                recv_ref.at[local, :, pl.ds(0, width)], x_all.at[pl.ds(0, rows)], load_sem.at[0]),
-            pltpu.make_async_copy(
-                recv_ref.at[local, :, pl.ds(width, width)], dy_all.at[pl.ds(0, rows)], load_sem.at[1]),
-            pltpu.make_async_copy(
-                recv_ref.at[local, :, pl.ds(2 * width, 2 * slab + 128)], side, load_sem.at[2]),
-        ]
+        second_hop_arrived(local)
+        copies = []
+        for way in range(2):
+            here = pl.ds(way * half_width, half_width)
+            for at, (target, low, size) in enumerate((
+                (x_all.at[pl.ds(0, rows), here], 0, half_width),
+                (dy_all.at[pl.ds(0, rows), here], half_width, half_width),
+                (side.at[:, pl.ds(way * side_width, sent_width[way] - 2 * half_width)],
+                 2 * half_width, sent_width[way] - 2 * half_width),
+            )):
+                copies.append(pltpu.make_async_copy(
+                    recv_ref.at[local, :, pl.ds(offset[way] + low, size)], target, load_sem.at[way, at]))
         for copy in copies:
             copy.start()
         for copy in copies:
             copy.wait()
 
     def forward(local):
-        cut_x, cut_dy, weight_block = side[:, :slab], side[:, slab : 2 * slab], side[:, 2 * slab :]
+        side_rows = side[...]
+        weight_whole = side_rows[:, 2 * half_slab : 2 * half_slab + 1].astype(F32)
 
         def joiner(j):
             source = q // EXTRA * CELL + j * EXTRA + q % EXTRA
             return jnp.where(r == source, 1.0, 0.0).astype(BF16)
 
         for j in range(SLABS):
-            columns = pl.ds(j * slab, slab)
-            x_all[rows:, columns] = mm(joiner(j), cut_x).astype(BF16)
-            dy_all[rows:, columns] = mm(joiner(j), cut_dy).astype(BF16)
-        weight_whole = weight_block[:, 0:1].astype(F32)
-        weight_cut = mm(joiner(0), weight_block)[:, 64:65]
+            joined = mm(joiner(j), side_rows)
+            if j == 0:
+                weight_cut = joined[:, 2 * half_slab + 64 : 2 * half_slab + 65]
+            for way in range(2):
+                columns = pl.ds(way * half_width + j * half_slab, half_slab)
+                low = way * side_width
+                x_all[rows:, columns] = joined[:, low : low + half_slab].astype(BF16)
+                dy_all[rows:, columns] = joined[:, low + half_slab : low + 2 * half_slab].astype(BF16)
         weight = jnp.concatenate([weight_whole, weight_cut], axis=0)
         step = total // 3
         probs = []
@@ -291,7 +443,8 @@
         pieces = 2 * units // part
 
         def one(k, carry):
-            g = lax.rem(z + half + k, groups)
+            turn = lax.rem(k, 2)
+            g = lax.rem(z + half + groups + (1 - 2 * turn) * ((k + turn) // 2), groups)
             columns = pl.ds(pl.multiple_of(g * part, part), part)
             gu = (grad_scale * mm(x_all[:, columns], gu_grad[...], 0, 0)).astype(BF16)
             for s in range(pieces):
@@ -301,8 +454,14 @@
             return carry
 
         one(0, 0)
-        ring_step(local, 0)
-        lax.fori_loop(1, groups, one, 0)
+        for chain in chains[:2]:
+            hop(local, *chain, 0).start()
+        if half > 1:
+            one(1, 0)
+            one(2, 0)
+            for chain in chains[2:]:
+                hop(local, *chain, 0).start()
+        lax.fori_loop(min(half * 2 - 1, 3), groups, one, 0)
 
     def input_grads(local):
         piece = rows // 2
@@ -327,12 +486,18 @@
     lax.fori_loop(1, owners, greet, 0)
     pl.semaphore_signal(barrier, inc=1, device_id=ring_right, device_id_type=MESH)
     pl.semaphore_signal(barrier, inc=1, device_id=ring_left, device_id_type=MESH)
-    pack(0, local_count, owners, routes_ref, weights_ref, count_ref, x_ref, dy_ref, send.at[0])
+    fill_stage()
     pl.semaphore_wait(barrier, owners + 1)
-    spread_out(send, recv_ref, own_sem, send_sem, recv_sem, 0)
-    pack(1, local_count, owners, routes_ref, weights_ref, count_ref, x_ref, dy_ref, send.at[1])
-    all_of(send, recv_ref, send_sem, recv_sem, 0).wait_send()
-    spread_out(send, recv_ref, own_sem, send_sem, recv_sem, 1)
+    first_hop()
+    for way in range(2):
+        for copy in first_hop_copies(way):
+            copy.wait_recv()
+        pack_way(0, way)
+    second_hop(0)
+    for way in range(2):
+        pack_way(1, way)
+    second_hop_sent(0)
+    second_hop(1)
 
     load_weights(0, False)
     load_rows(0)
@@ -358,12 +523,15 @@
         wait_own(back_send, back_recv, back_own_sem, local)
     combine(local_count, owners, routes_ref, [back_recv.at[i] for i in range(local_count)], dx_ref, prob_ref)
     ring_end(1)
-    all_of(send, recv_ref, send_sem, recv_sem, 1).wait_send()
+    second_hop_sent(1)
+    for way in range(2):
+        for copy in first_hop_copies(way):
+            copy.wait_send()
     for local in range(local_count):
         all_of(back_send, back_recv, back_send_sem, back_recv_sem, local).wait_send()
-        for step in range(half):
-            hop(local, step, True).wait_send()
-            hop(local, step, False).wait_send()
+        for chain in chains:
+            for step in range(hops_of(*chain)):
+                hop(local, *chain, step).wait_send()
 
 
 def combine(local_count, owners, routes_ref, back_refs, dx_ref, prob_ref):
@@ -376,7 +544,8 @@
     probs = [0.0] * top_k
     for local in range(local_count):
         back_ref = back_refs[local]
-        wanted, spread, place, whole, cut = cell_tables(routes_t, local, local_count, owners)
+        wanted = iota((owners, tokens), 0) * local_count + local
+        spread, place, whole, cut = cell_tables(routes_t, wanted)
         dx = dx + mm(jnp.where(whole, 1.0, 0.0).astype(BF16), back_ref[:, :width], 0, 0)
         for j in range(SLABS):
             here = jnp.where(cut & (place // EXTRA == j), 1.0, 0.0).astype(BF16)
@@ -395,6 +564,13 @@
         prob_ref[k : k + 1, :] = probs[k]
 
 
+def finish_kernel(prob_ref, *refs):
+    count = len(refs) // 2
+    for source, target in zip(refs[:count], refs[count : 2 * count]):
+        target[...] = source[...]
+    refs[-1][...] = prob_ref[...].T.astype(BF16)
+
+
 def vmem():
     return pl.BlockSpec(memory_space=pltpu.VMEM)
 
@@ -412,26 +588,32 @@
     extra = owners * EXTRA
     slab = width // SLABS
     half = groups // 2
-    send_width = 2 * width + 2 * slab + 128
+    send_width = width + slab + 128
+    across = 1 << ((owners // 2).bit_length() // 2)
+    longest = max(across, owners // 2 // across)
     back_width = width + slab + 128
     part = width // groups
     block = 3 * units
     dma = pltpu.SemaphoreType.DMA
+    routes_t = routes.T
+    meta = jnp.concatenate([routes_t.astype(BF16), route_weights.T], axis=0)
     in_grad, prob_t, gate_grad, up_grad, down_grad, _ = pl.pallas_call(
-        functools.partial(whole_kernel, grad_scale),
+        functools.partial(whole_kernel, grad_scale, across),
         out_shape=(
             jax.ShapeDtypeStruct((tokens, width), BF16),
             jax.ShapeDtypeStruct((top_k, tokens), F32),
             jax.ShapeDtypeStruct((local_count, part, units), BF16),
             jax.ShapeDtypeStruct((local_count, part, units), BF16),
             jax.ShapeDtypeStruct((local_count, units, part), BF16),
-            jax.ShapeDtypeStruct((local_count, rows, send_width), BF16),
+            jax.ShapeDtypeStruct((local_count, rows, 2 * send_width - 128), BF16),
         ),
         in_specs=[vmem(), vmem(), pl.BlockSpec(memory_space=pltpu.SMEM), vmem(), vmem()]
         + [pl.BlockSpec(memory_space=pl.ANY)] * 3,
         out_specs=(vmem(), vmem(), vmem(), vmem(), vmem(), pl.BlockSpec(memory_space=pl.ANY)),
         scratch_shapes=[
-            pltpu.VMEM((local_count, rows, send_width), BF16),
+            pltpu.VMEM((2, longest, tokens, width), BF16),
+            pltpu.VMEM((2, longest, 2 * top_k, tokens), BF16),
+            pltpu.VMEM((local_count, 2, rows, send_width), BF16),
             pltpu.VMEM((rows + extra, width), BF16),
             pltpu.VMEM((rows + extra, width), BF16),
             pltpu.VMEM((rows, 2 * slab + 128), BF16),
@@ -443,17 +625,24 @@
             pltpu.VMEM((local_count, half, block, part), BF16),
             pltpu.VMEM((local_count, half, block, part), BF16),
             pltpu.VMEM((local_count, rows, back_width), BF16),
-            pltpu.VMEM((local_count, rows, back_width), BF16),
-            dma((3,)), dma((2,)), dma((2,)), dma((2,)), dma((2,)), dma((2,)), dma((2,)),
-            dma((3,)), dma((2, 2, half)), dma((2, 2, half)),
+            dma((2,)), dma((2,)), dma((2,)), dma((2,)),
+            dma((2, 3)), dma((2, 2)), dma((2, 2)), dma((2, 2)), dma((2,)), dma((2,)), dma((2,)),
+            dma((3,)), dma((2, 2, 2, half)), dma((2, 2, 2, half)),
         ],
         compiler_params=pltpu.CompilerParams(
             vmem_limit_bytes=VMEM_LIMIT, collective_id=0, has_side_effects=True
         ),
         name="whole",
-    )(routes.T, route_weights.T, response_counts, inputs, out_grad, gate_weight, up_weight, down_weight)
-    route_weight_grad = prob_t.T.astype(BF16)
-    return in_grad, gate_grad, up_grad, down_grad, route_weight_grad
+    )(routes_t, meta, response_counts, inputs, out_grad, gate_weight, up_weight, down_weight)
+    results = (in_grad, gate_grad, up_grad, down_grad)
+    return pl.pallas_call(
+        finish_kernel,
+        out_shape=tuple(jax.ShapeDtypeStruct(a.shape, BF16) for a in results)
+        + (jax.ShapeDtypeStruct((tokens, top_k), BF16),),
+        in_specs=[vmem()] * 5,
+        out_specs=tuple([vmem()] * 5),
+        name="finish",
+    )(prob_t, *results)
 
 
 def solution(mesh):

time: 196 us -> 181 us (0.923)
  Pallas kernels: 184 us -> 174 us
  local copies, waits for them, and re-layouts: 7.21 us -> 1.41 us
    pallas_call x1 -> x2, Pallas kernels: 184 us -> 174 us  [the longest x1 171 us: shards(): pl.pallas_call(functools.partial(whole_kernel, grad_scale, across), out_s...]
    unnamed x4 -> x0, local copies, waits for them, and re-layouts: 7.21 us -> none
where the time goes in v3:
time: 181 us; the launch traced here: 178 us
  Pallas kernels  174 us (96%)
  other arithmetic  1.97 us (1%)
    pallas_call x1, Pallas kernels, shards(): pl.pallas_call(functools.partial(whole_kernel, grad_scale, across), out_s...  171 us

profile of v3, /device:TPU:9, one launch (start us, length us, event | category | flops | bytes accessed | tf_op | source)
XLA Modules:
  0.0 178.4 jit_solution(13025638849274447619)
XLA Ops:
  1.3 0.7 bitcast_convert_fusion
  2.0 1.3 pad_maximum_fusion.meta_ref
  3.2 171.1 %whole.1 = (bf16[128,2048]{1,0:T(8,128)(2,1)}, f32[8,128]{1,0:T(8,128)}, bf16[2,256,384]{2,1,0:T(8,128)(2,1)}, bf16[2,256,384]{2,1,0:T(8,128)(2,1)}, bf16[2,384,...) custom-call(s32[8,128]{1,0:T(8,128)} %bitcast.3, bf16[16,128]{1,0:T(8,128)(2,1)} %pad_maximum_fusion.meta_ref, ...), custom_call_target="tpu_custom_call" | custom-call | tf_op jit(solution)/shard_map/whole/pallas_call | solution.py:600
  174.4 2.6 %finish.1 = (bf16[128,2048]{1,0:T(8,128)(2,1)}, bf16[2,256,384]{2,1,0:T(8,128)(2,1)}, bf16[2,256,384]{2,1,0:T(8,128)(2,1)}, bf16[2,384,256]{2,1,0:T(8,128)(2,1)}, bf16[128,8]{1,0:T(8,128)(2,1)}) custom-call(f32[8,128]{1,0:T(8,128)} %get-tuple-element.10.prob_ref, bf16[128,2048]{1,0:T(8,128)(2,1)} %get-tuple-element.11.refs_0_, ...), custom_call_target="tpu_custom_call" | custom-call | tf_op jit(solution)/shard_map/finish/pallas_call | solution.py:638
  177.0 1.4 copy.13

commit v4 on v3

--- a/solution.py
+++ b/solution.py
@@ -44,7 +44,7 @@
     return spread, place, whole, cut
 
 
-def pack(wanted, meta, rows_in, out_ref, top):
+def pack(wanted, meta, rows_in, out_ref, top, part):
     tokens = meta.shape[1]
     width = rows_in.shape[1]
     slab = width // 2 // SLABS
@@ -57,7 +57,10 @@
             routes_t[k : k + 1, :] == wanted, weights_t[k : k + 1, :], 0.0
         )
     weight_rows = mm(spread, combine_weights.astype(BF16))
-    out_ref[:, :width] = mm(jnp.where(whole, 1.0, 0.0).astype(BF16), rows_in).astype(BF16)
+    here = pl.ds(part * (width // 2), width // 2)
+    out_ref[:, here] = mm(jnp.where(whole, 1.0, 0.0).astype(BF16), rows_in[:, here]).astype(BF16)
+    if part == 0:
+        return
     picks = [jnp.where(cut & (place // EXTRA == j), 1.0, 0.0).astype(BF16) for j in range(SLABS)]
     slabs = [
         jnp.concatenate(
@@ -143,39 +146,47 @@
         for c in range(pieces):
             for way in range(2):
 
-                def one(i, carry, way=way, columns=pl.ds(c * size, size)):
+                def one(i, carry, way=way, columns=pl.ds(c * size, size), part=c * 2 // pieces):
                     s = lax.rem(mine[way] + i, sources[way])
                     pltpu.make_async_remote_copy(
                         src_ref=stage.at[way, mine[way], :, columns],
                         dst_ref=stage.at[way, mine[way], :, columns],
-                        send_sem=stage_send_sem.at[way], recv_sem=stage_recv_sem.at[way],
+                        send_sem=stage_send_sem.at[way, part], recv_sem=stage_recv_sem.at[way, part],
                         device_id=(z, source_index(way, s)), device_id_type=MESH,
                     ).start()
                     return carry
 
                 lax.fori_loop(1, sources[way], one, 0)
 
-    def first_hop_copies(way):
+    def first_hop_copies(way, part):
+        if sources[way] == 1:
+            return []
         others = pl.ds(0, sources[way] - 1)
-        return [
+        rows_part = stage.at[way, others, :, pl.ds(part * half_width, half_width)]
+        copies = [
             pltpu.make_async_remote_copy(
-                src_ref=array.at[way, others], dst_ref=array.at[way, others],
-                send_sem=sends.at[way], recv_sem=recvs.at[way],
+                src_ref=rows_part, dst_ref=rows_part,
+                send_sem=stage_send_sem.at[way, part], recv_sem=stage_recv_sem.at[way, part],
                 device_id=beside, device_id_type=MESH,
             )
-            for array, sends, recvs in (
-                (meta, meta_send_sem, meta_recv_sem), (stage, stage_send_sem, stage_recv_sem),
+        ]
+        if part == 0:
+            copies.append(
+                pltpu.make_async_remote_copy(
+                    src_ref=meta.at[way, others], dst_ref=meta.at[way, others],
+                    send_sem=meta_send_sem.at[way], recv_sem=meta_recv_sem.at[way],
+                    device_id=beside, device_id_type=MESH,
+                )
             )
-            if sources[way] > 1
-        ]
-
-    def pack_way(local, way):
+        return copies
+
+    def pack_way(local, way, part):
         count = targets[way]
         wanted = target_index(way, iota((count, tokens), 0)) * local_count + local
 
         def one(s, carry):
             here = pl.ds(pl.multiple_of(s * count * CELL, CELL), count * CELL)
-            pack(wanted, meta[way, s], stage[way, s], send.at[local, way, here], meta.shape[2] // 2)
+            pack(wanted, meta[way, s], stage.at[way, s], send.at[local, way, here], meta.shape[2] // 2, part)
             return carry
 
         lax.fori_loop(0, sources[way], one, 0)
@@ -189,8 +200,8 @@
             ],
         )
 
-    def second_hop(local):
-        for way in range(2):
+    def second_hop(local, part):
+        for way in range(2 * part):
 
             def keep(s, carry, way=way):
                 a, b = cell_copy(local, way, s, my_target[way], pl.ds(0, sent_width[way]))
@@ -198,13 +209,15 @@
                 return carry
 
             lax.fori_loop(0, sources[way], keep, 0)
-        pieces = 4
+        pieces = 2 + part
         for c in range(pieces):
 
             def one(k, carry, ways=(0, 1), c=c):
                 for way in ways:
-                    tiles = sent_width[way] // 128
-                    low, high = tiles * c // pieces * 128, tiles * (c + 1) // pieces * 128
+                    first = half_width // 128 * part
+                    tiles = (sent_width[way] // 128 if part else half_width // 128) - first
+                    low = (first + tiles * c // pieces) * 128
+                    high = (first + tiles * (c + 1) // pieces) * 128
                     others = targets[way] - 1
                     d = lax.rem(my_target[way] + 1 + lax.rem(k, others), targets[way])
                     a, b = cell_copy(local, way, k // others, d, pl.ds(low, high - low))
@@ -489,29 +502,32 @@
     fill_stage()
     pl.semaphore_wait(barrier, owners + 1)
     first_hop()
-    for way in range(2):
-        for copy in first_hop_copies(way):
-            copy.wait_recv()
-        pack_way(0, way)
-    second_hop(0)
-    for way in range(2):
-        pack_way(1, way)
+    for part in range(2):
+        for way in range(2):
+            for copy in first_hop_copies(way, part):
+                copy.wait_recv()
+            pack_way(0, way, part)
+        second_hop(0, part)
+    for part in range(2):
+        for way in range(2):
+            pack_way(1, way, part)
     second_hop_sent(0)
-    second_hop(1)
+    second_hop(1, 0)
+    second_hop(1, 1)
 
     load_weights(0, False)
     load_rows(0)
     forward(0)
     weight_grads(0)
     input_grads(0)
-    spread_out(back_send, back_recv, back_own_sem, back_send_sem, back_recv_sem, 0)
     load_weights(1, True)
-    for step in range(1, half):
+    for step in range(1, half - 1):
         ring_step(0, step)
-
     load_weights(1, False)
     load_rows(1)
+    spread_out(back_send, back_recv, back_own_sem, back_send_sem, back_recv_sem, 0)
     forward(1)
+    ring_step(0, half - 1)
     weight_grads(1)
     input_grads(1)
     spread_out(back_send, back_recv, back_own_sem, back_send_sem, back_recv_sem, 1)
@@ -525,7 +541,7 @@
     ring_end(1)
     second_hop_sent(1)
     for way in range(2):
-        for copy in first_hop_copies(way):
+        for copy in first_hop_copies(way, 0) + first_hop_copies(way, 1):
             copy.wait_send()
     for local in range(local_count):
         all_of(back_send, back_recv, back_send_sem, back_recv_sem, local).wait_send()
@@ -625,7 +641,7 @@
             pltpu.VMEM((local_count, half, block, part), BF16),
             pltpu.VMEM((local_count, half, block, part), BF16),
             pltpu.VMEM((local_count, rows, back_width), BF16),
-            dma((2,)), dma((2,)), dma((2,)), dma((2,)),
+            dma((2, 2)), dma((2, 2)), dma((2,)), dma((2,)),
             dma((2, 3)), dma((2, 2)), dma((2, 2)), dma((2, 2)), dma((2,)), dma((2,)), dma((2,)),
             dma((3,)), dma((2, 2, 2, half)), dma((2, 2, 2, half)),
         ],

time: 181 us -> 176 us (0.972)
  Pallas kernels: 174 us -> 170 us
    pallas_call x1, Pallas kernels: 171 us -> 167 us  [shards(): pl.pallas_call(functools.partial(whole_kernel, grad_scale, across), out_s...]
where the time goes in v4:
time: 176 us; the launch traced here: 174 us
  Pallas kernels  170 us (97%)
  other arithmetic  1.97 us (1%)
    pallas_call x1, Pallas kernels, shards(): pl.pallas_call(functools.partial(whole_kernel, grad_scale, across), out_s...  167 us

profile of v4, /device:TPU:9, one launch (start us, length us, event | category | flops | bytes accessed | tf_op | source)
XLA Modules:
  0.0 174.3 jit_solution(1608406876267808988)
XLA Ops:
  1.3 0.7 bitcast_convert_fusion
  2.0 1.3 pad_maximum_fusion.meta_ref
  3.2 167.0 %whole.1 = (bf16[128,2048]{1,0:T(8,128)(2,1)}, f32[8,128]{1,0:T(8,128)}, bf16[2,256,384]{2,1,0:T(8,128)(2,1)}, bf16[2,256,384]{2,1,0:T(8,128)(2,1)}, bf16[2,384,...) custom-call(s32[8,128]{1,0:T(8,128)} %bitcast.3, bf16[16,128]{1,0:T(8,128)(2,1)} %pad_maximum_fusion.meta_ref, ...), custom_call_target="tpu_custom_call" | custom-call | tf_op jit(solution)/shard_map/whole/pallas_call | solution.py:616
  170.3 2.6 %finish.1 = (bf16[128,2048]{1,0:T(8,128)(2,1)}, bf16[2,256,384]{2,1,0:T(8,128)(2,1)}, bf16[2,256,384]{2,1,0:T(8,128)(2,1)}, bf16[2,384,256]{2,1,0:T(8,128)(2,1)}, bf16[128,8]{1,0:T(8,128)(2,1)}) custom-call(f32[8,128]{1,0:T(8,128)} %get-tuple-element.10.prob_ref, bf16[128,2048]{1,0:T(8,128)(2,1)} %get-tuple-element.11.refs_0_, ...), custom_call_target="tpu_custom_call" | custom-call | tf_op jit(solution)/shard_map/finish/pallas_call | solution.py:654
  172.9 1.4 copy.13
